TPU v7x, 512 devices: a whole 4x8x8 slice. The times are simulated.
512 devices in a mesh: dp: 4 (over z_lo), seq: 16 (over y, z_hi), tensor: 8 (over x, core).
Axes of the slice: x: 4, y: 8, z: 8 (z_hi: 2, z_lo: 4; z = z_hi * 4 + z_lo), core: 2. Of those that a mesh axis runs over, the one named last changes fastest.
Arguments:
- inputs: bfloat16 [4, 4096, 1536], P('dp', 'seq', 'tensor'), may hold values from -6 to 6
- targets: bfloat16 [4, 4096, 1536], P('dp', 'seq', 'tensor'), may hold values from -6 to 6
- block_mix: bfloat16 [256, 256], replicated, may hold values from -0.375 to 0.375
- cross_mix: bfloat16 [16, 16], replicated, may hold values from -1.5 to 1.5
- twiddle_in: float32 [16, 256], P('seq'), may hold values from 0.5 to 1.5
- twiddle_out: float32 [16, 256], P(None, 'seq'), may hold values from 0.5 to 1.5
- norm_gain: float32 [1536], replicated, may hold values from 0.3 to 2.8
- w_gate: bfloat16 [1536, 3072], P(None, 'tensor'), may hold values from -0.15625 to 0.15625
- w_up: bfloat16 [1536, 3072], P(None, 'tensor'), may hold values from -0.15625 to 0.15625
- w_down: bfloat16 [1536, 3072], P(None, 'tensor'), may hold values from -0.109375 to 0.109375
Outputs:
- output: bfloat16 [4, 4096, 1536], P('dp', 'seq', 'tensor')
- d_input: bfloat16 [4, 4096, 1536], P('dp', 'seq', 'tensor')
- grad_down: float32 [1536, 3072], P(('dp', 'seq'), 'tensor')
All inputs are finite; a program needn't handle non-finite values.
Results may differ from a plain program's by a relative error of at most 0.022.
Values may be sent and summed in bfloat16 or wider, within the bound.
A program may use at most 64 MiB of HBM per device.

v0:
```python
import jax
import jax.numpy as jnp
from jax import lax
from jax.sharding import PartitionSpec as P

BLOCK = 256
BLK_DEV = 1


def body(
    inputs, targets, block_mix, cross_mix, twiddle_in, twiddle_out, norm_gain, w_gate, w_up, w_down
):
    tok_rows = inputs.shape[1]
    channels = inputs.shape[2]
    contract_last = (((1,), (1,)), ((), ()))
    contract_first = (((0,), (0,)), ((), ()))
    source = inputs[0]
    local_x = source.reshape(BLK_DEV, BLOCK, channels)
    section_mix = (
        jnp.einsum("pqc,qj->pjc", local_x, block_mix, preferred_element_type=jnp.float32)
        * twiddle_in[:, :, None]
    ).astype(jnp.bfloat16)
    mixed_cols = (
        jnp.einsum(
            "pjc,pk->kjc",
            lax.all_to_all(section_mix, "seq", split_axis=1, concat_axis=0, tiled=True),
            cross_mix,
            preferred_element_type=jnp.float32,
        )
        * twiddle_out[:, :, None]
    )
    mixed_rows = lax.all_to_all(
        mixed_cols.astype(jnp.bfloat16), "seq", split_axis=0, concat_axis=1, tiled=True
    )
    res_f = source.astype(jnp.float32) + mixed_rows.reshape(tok_rows, channels).astype(jnp.float32)
    residual = res_f.astype(jnp.bfloat16)
    res_f = residual.astype(jnp.float32)
    gathered = lax.all_gather(residual, "tensor", axis=1, tiled=True)
    full_d = gathered.shape[1]
    whole_f = gathered.astype(jnp.float32)
    inv_rms = lax.rsqrt(jnp.mean(whole_f * whole_f, axis=1, keepdims=True) + 1e-05)
    normed = (whole_f * inv_rms * norm_gain).astype(jnp.bfloat16)
    gate_pre = jnp.dot(normed, w_gate, preferred_element_type=jnp.float32)
    up_pre = jnp.dot(normed, w_up, preferred_element_type=jnp.float32)
    sigmoid_gate = jax.nn.sigmoid(gate_pre)
    hidden = (gate_pre * sigmoid_gate * up_pre).astype(jnp.bfloat16)
    partial_value = lax.dot_general(
        hidden, w_down, contract_last, preferred_element_type=jnp.float32
    )
    projected = lax.psum_scatter(
        partial_value.astype(jnp.bfloat16), "tensor", scatter_dimension=1, tiled=True
    ).astype(jnp.float32)
    summed_out = res_f + projected
    output = summed_out.astype(jnp.bfloat16)[None]
    cotangent = (summed_out - targets[0].astype(jnp.float32)).astype(jnp.bfloat16)
    cot_full = lax.all_gather(cotangent, "tensor", axis=1, tiled=True)
    grad_down = lax.psum_scatter(
        lax.dot_general(cot_full, hidden, contract_first, preferred_element_type=jnp.float32),
        ("dp", "seq"),
        scatter_dimension=0,
        tiled=True,
    )
    d_hidden = jnp.dot(cot_full, w_down, preferred_element_type=jnp.float32)
    d_gate = (d_hidden * up_pre * sigmoid_gate * (1.0 + gate_pre * (1.0 - sigmoid_gate))).astype(
        jnp.bfloat16
    )
    d_up = (d_hidden * gate_pre * sigmoid_gate).astype(jnp.bfloat16)
    partial_dn = lax.dot_general(d_gate, w_gate, contract_last, preferred_element_type=jnp.float32)
    partial_dn = partial_dn + lax.dot_general(
        d_up, w_up, contract_last, preferred_element_type=jnp.float32
    )
    tensor_pos = lax.axis_index("tensor")
    d_normed = lax.psum_scatter(
        partial_dn.astype(jnp.bfloat16), "tensor", scatter_dimension=1, tiled=True
    ).astype(jnp.float32)
    gain_local = lax.dynamic_slice_in_dim(norm_gain, tensor_pos * channels, channels, 0)
    scaled = gain_local * d_normed
    unit_local = res_f * inv_rms
    product_sum = lax.psum(jnp.sum(scaled * unit_local, axis=1, keepdims=True), "tensor")
    correction = product_sum / full_d
    d_resid_f = cotangent.astype(jnp.float32) + inv_rms * (scaled - unit_local * correction)
    d_resid = d_resid_f.astype(jnp.bfloat16)
    back_weighted = (
        lax.all_to_all(
            d_resid.reshape(BLK_DEV, BLOCK, channels),
            "seq",
            split_axis=1,
            concat_axis=0,
            tiled=True,
        ).astype(jnp.float32)
        * twiddle_out[:, :, None]
    ).astype(jnp.bfloat16)
    back_section = jnp.einsum(
        "kjc,pk->pjc", back_weighted, cross_mix, preferred_element_type=jnp.float32
    )
    back_rows = lax.all_to_all(
        back_section.astype(jnp.bfloat16), "seq", split_axis=0, concat_axis=1, tiled=True
    )
    back_scaled = (back_rows.astype(jnp.float32) * twiddle_in[:, :, None]).astype(jnp.bfloat16)
    d_mix = jnp.einsum(
        "pjc,qj->pqc", back_scaled, block_mix, preferred_element_type=jnp.float32
    ).reshape(tok_rows, channels)
    d_input = (d_resid.astype(jnp.float32) + d_mix).astype(jnp.bfloat16)[None]
    return (output, d_input, grad_down)


def solution(mesh):
    return jax.shard_map(
        body,
        mesh=mesh,
        in_specs=(
            P("dp", "seq", "tensor"),
            P("dp", "seq", "tensor"),
            P(),
            P(),
            P("seq", None),
            P(None, "seq"),
            P(),
            P(None, "tensor"),
            P(None, "tensor"),
            P(None, "tensor"),
        ),
        out_specs=(P("dp", "seq", "tensor"), P("dp", "seq", "tensor"), P(("dp", "seq"), "tensor")),
        check_vma=False,
    )
```

profile of v0, /device:TPU:92, one launch (start us, length us, event | category | flops | bytes accessed | tf_op | source)
XLA Modules:
  0.0 549.2 jit_solution(2111071353783990135)
XLA Ops:
  7.2 0.0 copy-start
  7.2 0.0 copy-start.10
  7.2 0.0 copy-start.11
  7.2 1.2 fusion.10
  8.4 0.2 copy.27
  8.6 0.6 broadcast.42
  9.2 1.4 reduce
  10.6 0.8 reshape.73
  11.4 14.9 %all-to-all-start = ((bf16[16,2,1536]{2,1,0:T(2,128)(2,1)}), bf16[16,2,1536]{2,1,0:T(2,128)(2,1)S(1)}, u32[]{:S(2)}, u32[]{:S(2)}) async-start(bf16[16,2,1536]{2,1,0:T(2,128)(2,1)} %reshape.73), calls=%async_computation | async-start | bytes 196608 | tf_op jit(solution)/shard_map/all_to_all | solution.py:26
  26.3 0.0 reduce-scatter.7.cloned.1.call-start
  26.4 0.0 copy-done.10
  26.4 0.1 copy.30
  26.5 10.2 %all-to-all-done = bf16[16,2,1536]{2,1,0:T(2,128)(2,1)S(1)} async-done(((bf16[16,2,1536]{2,1,0:T(2,128)(2,1)}), bf16[16,2,1536]{2,1,0:T(2,128)(2,1)S(1)}, u32[]{:S(2)}, u32[]{:S(2)}) %all-to-all-start) | async-done | bytes 98336 | tf_op jit(solution)/shard_map/all_to_all | solution.py:26
  36.7 0.2 reshape.74
  36.9 0.0 copy-done.11
  36.9 0.2 fusion.5
  37.2 16.1 %all_to_all.19 = bf16[16,16,192]{2,1,0:T(8,128)(2,1)S(1)} all-to-all(bf16[16,16,192]{2,1,0:T(8,128)(2,1)S(1)} %copy.31), channel_id=1, replica_groups=mesh['dp'=4,'seq'=16,'tensor'=8] {'seq'}, dimensions={0} | all-to-all | bytes 196608 | tf_op jit(solution)/shard_map/all_to_all | solution.py:32
  53.3 0.0 copy-start.4
  53.3 0.0 copy-start.13
  53.3 0.1 copy.32
  53.4 0.0 copy-done.7
  53.5 12.4 %all_gather.6 = bf16[256,1536]{0,1:T(8,128)(2,1)S(1)} all-gather(bf16[256,192]{0,1:T(8,128)(2,1)S(1)} %add_convert_fusion), channel_id=1, replica_groups=mesh['dp'=4,'seq'=16,'tensor'=8] {'tensor'}, dimensions={1}, use_global_device_ids=true | all-gather | bytes 884736 | tf_op jit(solution)/shard_map/all_gather | solution.py:38
  65.9 0.2 fusion.1
  66.1 0.0 copy-done.4
  66.1 0.0 copy-done.13
  66.1 1.1 fusion.17
  67.2 0.0 copy-done
  67.3 0.0 copy-start.2
  67.3 0.0 copy-start.1
  67.3 1.9 multiply_convert_fusion.2
  69.2 0.0 copy-done.2
  69.2 1.5 convolution_convert_fusion
  70.6 0.0 reduce-scatter.7.cloned.1.call-update
  70.7 0.0 reduce-scatter.9.cloned.1.call-start
  70.7 29.3 %reduce-scatter.7.cloned.1.call-done = bf16[256,192]{0,1:T(8,128)(2,1)} async-done(((bf16[256,1536]{0,1:T(8,128)(2,1)}), bf16[256,192]{0,1:T(8,128)(2,1)}) %reduce-scatter.7.cloned.1.call-update) | async-done | bytes 98320 | tf_op jit(solution)/shard_map/reduce_scatter | solution.py:50
  100.1 1.6 fusion.25
  101.6 17.0 %all_gather.7 = bf16[256,1536]{0,1:T(8,128)(2,1)S(1)} all-gather(bf16[256,192]{0,1:T(8,128)(2,1)S(1)} %get-tuple-element.3), channel_id=1, replica_groups=mesh['dp'=4,'seq'=16,'tensor'=8] {'tensor'}, dimensions={1}, use_global_device_ids=true | all-gather | bytes 884736 | tf_op jit(solution)/shard_map/all_gather | solution.py:56
  118.6 0.6 fusion.39
  119.2 0.4 copy-done.3
  119.6 0.4 copy-done.5
  120.0 0.1 copy-done.8
  120.1 0.7 fusion.24
  120.8 1.6 fusion
  122.4 0.0 reduce-scatter.9.cloned.1.call-update
  122.4 0.0 reduce-scatter.11.cloned.1.call-start
  122.4 2.0 fusion.40
  124.4 0.0 reduce-scatter.11.cloned.1.call-update
  124.5 0.8 dynamic_slice.3
  125.2 30.3 %reduce-scatter.9.cloned.1.call-done = bf16[256,192]{0,1:T(8,128)(2,1)} async-done(((bf16[256,1536]{0,1:T(8,128)(2,1)}), bf16[256,192]{0,1:T(8,128)(2,1)}) %reduce-scatter.9.cloned.1.call-update) | async-done | bytes 98320 | tf_op jit(solution)/shard_map/reduce_scatter | solution.py:73
  155.5 1.0 fusion.19
  156.5 12.1 %psum.7 = f32[256,1]{0,1:T(1,128)S(1)} all-reduce(f32[256,1]{0,1:T(1,128)S(1)} %bitcast.75), channel_id=1, replica_groups=mesh['dp'=4,'seq'=16,'tensor'=8] {'tensor'}, use_global_device_ids=true, to_apply=%region_4.0 | all-reduce | flops 256 | bytes 2048 | tf_op jit(solution)/shard_map/psum | solution.py:79
  168.6 1.0 fusion.23
  169.6 0.2 copy.33
  169.8 1.4 reduce.1
  171.3 0.2 reshape.75
  171.4 22.7 %all_to_all.40 = bf16[16,2,1536]{2,1,0:T(2,128)(2,1)S(1)} all-to-all(bf16[16,2,1536]{2,1,0:T(2,128)(2,1)S(1)} %reshape.75), channel_id=1, replica_groups=mesh['dp'=4,'seq'=16,'tensor'=8] {'seq'}, dimensions={0} | all-to-all | bytes 196608 | tf_op jit(solution)/shard_map/all_to_all | solution.py:84
  194.2 0.2 reshape.76
  194.4 0.0 copy-start.6
  194.4 0.0 copy-start.12
  194.4 0.3 fusion.9
  194.8 17.3 %all_to_all.41 = bf16[16,16,192]{2,1,0:T(8,128)(2,1)S(1)} all-to-all(bf16[16,16,192]{2,1,0:T(8,128)(2,1)S(1)} %copy.36), channel_id=1, replica_groups=mesh['dp'=4,'seq'=16,'tensor'=8] {'seq'}, dimensions={0} | all-to-all | bytes 196608 | tf_op jit(solution)/shard_map/all_to_all | solution.py:96
  212.1 0.1 copy.37
  212.3 0.9 fusion.11
  213.1 329.5 %reduce-scatter.11.cloned.1.call-done = f32[24,384]{1,0:T(8,128)} async-done(((f32[1536,384]{1,0:T(8,128)}), f32[24,384]{1,0:T(8,128)}) %reduce-scatter.11.cloned.1.call-update) | async-done | bytes 36880
  (19 shorter events, 0.3 us)
Async XLA Ops:
  7.2 60.1 %copy-start = (bf16[1536,384]{1,0:T(8,128)(2,1)S(1)}, bf16[1536,384]{1,0:T(8,128)(2,1)}, u32[]{:S(2)}) copy-start(bf16[1536,384]{1,0:T(8,128)(2,1)} %param.18) | copy-start | bytes 3538948
  7.2 19.2 %copy-start.10 = (f32[16,16]{1,0:T(8,128)S(1)}, f32[16,16]{1,0:T(8,128)}, u32[]{:S(2)}) copy-start(f32[16,16]{1,0:T(8,128)} %param.15) | copy-start | bytes 3076
  7.2 29.7 %copy-start.11 = (bf16[16,16]{1,0:T(8,128)(2,1)S(1)}, bf16[16,16]{1,0:T(8,128)(2,1)}, u32[]{:S(2)}) copy-start(bf16[16,16]{1,0:T(8,128)(2,1)} %param.13) | copy-start | bytes 1540
  11.4 25.2 %all-to-all-start = ((bf16[16,2,1536]{2,1,0:T(2,128)(2,1)}), bf16[16,2,1536]{2,1,0:T(2,128)(2,1)S(1)}, u32[]{:S(2)}, u32[]{:S(2)}) async-start(bf16[16,2,1536]{2,1,0:T(2,128)(2,1)} %reshape.73), calls=%async_computation | async-start | bytes 196608 | tf_op jit(solution)/shard_map/all_to_all | solution.py:26
  26.3 73.7 %reduce-scatter.7.cloned.1.call-start = ((), (), s32[]{:S(2)}) async-start(), calls=%async_computation.7 | async-start | bytes 884736 | tf_op jit(solution)/shard_map/reduce_scatter | solution.py:50
  26.4 27.0 %copy-start.7 = (bf16[1,256,192]{1,2,0:T(8,128)(2,1)S(1)}, bf16[1,256,192]{1,2,0:T(8,128)(2,1)}, u32[]{:S(2)}) copy-start(bf16[1,256,192]{1,2,0:T(8,128)(2,1)} %param.10) | copy-start | bytes 294916
  53.3 12.8 %copy-start.4 = (bf16[1536,384]{1,0:T(8,128)(2,1)S(1)}, bf16[1536,384]{1,0:T(8,128)(2,1)}, u32[]{:S(2)}) copy-start(bf16[1536,384]{1,0:T(8,128)(2,1)} %param.17) | copy-start | bytes 3538948
  53.3 12.8 %copy-start.13 = (f32[1536]{0:T(1024)S(1)}, f32[1536]{0:T(1024)}, u32[]{:S(2)}) copy-start(f32[1536]{0:T(1024)} %param.16) | copy-start | bytes 18436
  67.3 1.9 copy-start.2
  67.3 1.9 copy-start.1
  69.2 30.9 %copy-start.9 = (bf16[1,256,192]{1,2,0:T(8,128)(2,1)S(1)}, bf16[1,256,192]{1,2,0:T(8,128)(2,1)}, u32[]{:S(2)}) copy-start(bf16[1,256,192]{1,2,0:T(8,128)(2,1)} %param.11) | copy-start | bytes 294916
  70.7 84.8 %reduce-scatter.9.cloned.1.call-start = ((), (), s32[]{:S(2)}) async-start(), calls=%async_computation.8 | async-start | bytes 884736 | tf_op jit(solution)/shard_map/reduce_scatter | solution.py:73
  118.6 1.0 copy-start.3
  118.6 1.4 copy-start.5
  118.6 1.5 copy-start.8
  122.4 420.2 %reduce-scatter.11.cloned.1.call-start = ((), (), s32[]{:S(2)}) async-start(), calls=%async_computation.9 | async-start | bytes 2396160
  194.4 17.9 %copy-start.6 = (bf16[256,256]{1,0:T(8,128)(2,1)S(1)}, bf16[256,256]{1,0:T(8,128)(2,1)}, u32[]{:S(2)}) copy-start(bf16[256,256]{1,0:T(8,128)(2,1)} %param.12) | copy-start | bytes 393220
  194.4 17.9 %copy-start.12 = (f32[1,256]{1,0:T(1,128)S(1)}, f32[1,256]{1,0:T(1,128)}, u32[]{:S(2)}) copy-start(f32[1,256]{1,0:T(1,128)} %param.14) | copy-start | bytes 3076
Sparse Core Ops, SparseCore 0:
  70.8 29.2 reduce-scatter.6
  122.5 32.9 reduce-scatter.8
  158.9 383.7 reduce-scatter.10
where the time goes:
time: 550 us; the launch traced here: 549 us
  waiting for transfers between devices  399 us (73%)
  blocking collectives  97.6 us (18%)
  starting transfers between devices  15 us (3%)
  between operations  14 us (3%)
  matrix products  11.9 us (2%)
  other arithmetic  6.8 us (1%)
    unnamed x4, waiting for transfers between devices  330 us
    reduce_scatter x1, waiting for transfers between devices, body(): lax.psum_scatter(partial_dn.astype(jnp.bfloat16), 'tensor', scatter_dimen...  30.3 us
    reduce_scatter x1, waiting for transfers between devices, body(): lax.psum_scatter(partial_value.astype(jnp.bfloat16), 'tensor', scatter_di...  29.3 us
    all_to_all x1, blocking collectives, body(): lax.all_to_all(d_resid.reshape(BLK_DEV, BLOCK, channels), 'seq', split_ax...  22.7 us
    all_to_all x1, blocking collectives, body(): lax.all_to_all(back_section.astype(jnp.bfloat16), 'seq', split_axis=0, co...  17.3 us
    all_gather x1, blocking collectives, body(): cot_full = lax.all_gather(cotangent, 'tensor', axis=1, tiled=True)  17 us
    all_to_all x1, blocking collectives, body(): lax.all_to_all(mixed_cols.astype(jnp.bfloat16), 'seq', split_axis=0, conc...  16.1 us
    all_to_all x1, starting transfers between devices, body(): lax.all_to_all(section_mix, 'seq', split_axis=1, concat_axis=0, tiled=True)  14.9 us
  transfers between devices with their start and end apart: 4, of which 4 were waited for; matrix products, arithmetic and copies ran while one was open for 1% of the time, Pallas kernels for 0%

commit v1 on v0

v1 whole, which is shorter than its diff:
```python
import functools

import jax
import jax.numpy as jnp
from jax import lax
from jax.experimental import pallas as pl
from jax.experimental.pallas import tpu as pltpu
from jax.sharding import PartitionSpec as P

F32 = jnp.float32
BF16 = jnp.bfloat16
MESH = pl.DeviceIdType.MESH

TOK = 256
CH = 192
HID = 384
NSEQ = 16
NTEN = 8
POS = 16
D = 1536
GY = 256
GZ = HID - GY
ROWS = 24
EPS = 1e-05


def mm(a, b, ca=1, cb=0):
    return lax.dot_general(a, b, (((ca,), (cb,)), ((), ())), preferred_element_type=F32)


def eye(n, dtype=BF16):
    rows = lax.broadcasted_iota(jnp.int32, (n, n), 0)
    cols = lax.broadcasted_iota(jnp.int32, (n, n), 1)
    return jnp.where(rows == cols, 1.0, 0.0).astype(dtype)


def column_of(row):
    n = row.shape[1]
    return jnp.sum(eye(n, F32) * row, axis=1, keepdims=True)


def kernel(
    x_ref, tgt_ref, bm_ref, cm_ref, ti_ref, to_ref, gain_ref, wg_hbm, wu_hbm, wd_hbm,
    out_ref, din_ref, gd_ref,
    wg, wu, wd, wguT, wdT, kron, kronT,
    a1s, a1r, a2s, a2r, a3s, a3r, a4s, a4r,
    r1, r2, v1, v2,
    p1, p2, sb1, sb2, q1, q2, t1, t2, own, gate_s, up_s, hid_s, res_s,
    ya, yr, zb, zr, y2s, y2r, z2s, z2r,
    wsem, a_ss, a_rs, ag_ss, ag_rs, sib_ss, sib_rs, v_ss, v_rs,
    rsib_ss, rsib_rs, rs_ss, rs_rs, g_ss, g_rs,
):
    dp = lax.axis_index("dp")
    sq = lax.axis_index("seq")
    tn = lax.axis_index("tensor")
    x, c = tn // 2, tn % 2
    y, zh = sq // 2, sq % 2
    z = zh * 4 + dp

    def seq_dev(s):
        return (dp, s, tn)

    def ten_dev(t):
        return (dp, sq, t)

    def y_dev(yy):
        return (dp, yy * 2 + zh, tn)

    def z_dev(zz):
        return (lax.rem(zz, 4), y * 2 + zz // 4, tn)

    sent = []

    def send(src, dst, ss, rs, dev):
        cp = pltpu.make_async_remote_copy(
            src_ref=src, dst_ref=dst, send_sem=ss, recv_sem=rs, device_id=dev, device_id_type=MESH
        )
        cp.start()
        sent.append(cp)

    def wait_recv(buf, ss, rs):
        pltpu.make_async_remote_copy(
            src_ref=buf, dst_ref=buf, send_sem=ss, recv_sem=rs,
            device_id=(dp, sq, tn), device_id_type=MESH,
        ).wait_recv()

    barrier = pltpu.get_barrier_semaphore()

    def greet(dev):
        pl.semaphore_signal(barrier, inc=1, device_id=dev, device_id_type=MESH)

    def greet_seq(i, carry):
        greet(seq_dev(lax.rem(sq + i, NSEQ)))
        return carry

    def greet_ten(i, carry):
        greet(ten_dev(lax.rem(tn + i, NTEN)))
        return carry

    lax.fori_loop(1, NSEQ, greet_seq, 0)
    lax.fori_loop(1, NTEN, greet_ten, 0)
    for i in (1, 2, 3, 5, 6, 7):
        greet(z_dev(lax.rem(z + i, 8)))

    loads = []
    for n, (src, dst) in enumerate(((wg_hbm, wg), (wu_hbm, wu), (wd_hbm, wd))):
        cp = pltpu.make_async_copy(src, dst, wsem.at[n])
        cp.start()
        loads.append(cp)

    def all_to_all_send(n, src, dst):
        def one(i, carry):
            peer = lax.rem(sq + i, NSEQ)
            pltpu.make_async_remote_copy(
                src_ref=src.at[peer], dst_ref=dst.at[sq],
                send_sem=a_ss.at[n, peer], recv_sem=a_rs.at[n, sq],
                device_id=seq_dev(peer), device_id_type=MESH,
            ).start()
            return carry

        lax.fori_loop(1, NSEQ, one, 0)
        dst[sq] = src[sq]

    def all_to_all_wait(n, src, dst):
        def one(i, carry):
            peer = lax.rem(sq + i, NSEQ)
            wait_recv(dst.at[peer], a_ss.at[n, peer], a_rs.at[n, peer])
            return carry

        lax.fori_loop(1, NSEQ, one, 0)

    def all_to_all_done(n, src):
        def one(i, carry):
            peer = lax.rem(sq + i, NSEQ)
            pltpu.make_async_remote_copy(
                src_ref=src.at[peer], dst_ref=src.at[peer],
                send_sem=a_ss.at[n, peer], recv_sem=a_rs.at[n, peer],
                device_id=seq_dev(peer), device_id_type=MESH,
            ).wait_send()
            return carry

        lax.fori_loop(1, NSEQ, one, 0)

    tin = column_of(ti_ref[...])
    section = mm(bm_ref[...], x_ref[...], 0, 0) * tin
    a1s[...] = section.astype(BF16).reshape(NSEQ, POS, CH)

    pl.semaphore_wait(barrier, (NSEQ - 1) + (NTEN - 1) + 6)
    all_to_all_send(0, a1s, a1r)

    rows = lax.broadcasted_iota(jnp.int32, (TOK, NSEQ), 0)
    cols = lax.broadcasted_iota(jnp.int32, (TOK, NSEQ), 1)
    pick_block = jnp.where(rows // POS == cols, 1.0, 0.0)
    pick_pos = jnp.where(rows % POS == cols, 1.0, 0.0)
    cross = cm_ref[...]
    wide = mm(pick_block.astype(BF16), cross, 1, 1).astype(BF16)
    wide = mm(wide, pick_block.astype(BF16), 1, 1)
    wideT = mm(pick_block.astype(BF16), cross, 1, 0).astype(BF16)
    wideT = mm(wideT, pick_block.astype(BF16), 1, 1)
    big_r = lax.broadcasted_iota(jnp.int32, (TOK, TOK), 0)
    big_c = lax.broadcasted_iota(jnp.int32, (TOK, TOK), 1)
    same_pos = (big_r % POS) == (big_c % POS)
    kron[...] = jnp.where(same_pos, wide, 0.0).astype(BF16)
    kronT[...] = jnp.where(same_pos, wideT, 0.0).astype(BF16)
    tout_all = jnp.broadcast_to(to_ref[...][:, None, :], (NSEQ, POS, POS)).reshape(TOK, POS)
    tout = jnp.sum(tout_all * pick_pos, axis=1, keepdims=True)
    gains = gain_ref[...]
    gain_row = jnp.zeros((1, CH), F32)
    for r in range(NTEN):
        gain_row = gain_row + jnp.where(tn == r, gains[:, r * CH : (r + 1) * CH], 0.0)
    gain = column_of(gain_row)
    for cp in loads:
        cp.wait()
    eye_h = eye(HID)
    for k in range(4):
        block = slice(k * HID, (k + 1) * HID)
        wguT[k, 0:HID, :] = mm(eye_h, wg[block, :], 1, 1).astype(BF16)
        wguT[k, HID : 2 * HID, :] = mm(eye_h, wu[block, :], 1, 1).astype(BF16)
        wdT[k] = mm(eye_h, wd[block, :], 1, 1).astype(BF16)
    eye_c = eye(CH)
    eye_t = eye(TOK)
    tgtT = mm(eye_c, tgt_ref[...], 1, 1)

    all_to_all_wait(0, a1s, a1r)

    mixed = mm(kron[...], a1r[...].reshape(TOK, CH)) * tout
    a2s[...] = mixed.astype(BF16).reshape(NSEQ, POS, CH)
    all_to_all_send(1, a2s, a2r)
    all_to_all_wait(1, a2s, a2r)

    residual = (x_ref[...].astype(F32) + a2r[...].reshape(TOK, CH).astype(F32)).astype(BF16)
    res = mm(eye_c, residual, 1, 1)
    res_s[...] = res

    def share_row(n, buf, row):
        buf[tn] = jnp.broadcast_to(row, (8, TOK))

        def one(i, carry):
            peer = lax.rem(tn + i, NTEN)
            pltpu.make_async_remote_copy(
                src_ref=buf.at[tn], dst_ref=buf.at[tn],
                send_sem=v_ss.at[n, peer], recv_sem=v_rs.at[n, tn],
                device_id=ten_dev(peer), device_id_type=MESH,
            ).start()
            return carry

        lax.fori_loop(1, NTEN, one, 0)

    def sum_rows(n, buf):
        def one(i, carry):
            peer = lax.rem(tn + i, NTEN)
            wait_recv(buf.at[peer], v_ss.at[n, peer], v_rs.at[n, peer])
            return carry

        lax.fori_loop(1, NTEN, one, 0)
        return jnp.sum(buf[:, 0:1, :], axis=0)

    def rows_done(n, buf):
        def one(i, carry):
            peer = lax.rem(tn + i, NTEN)
            pltpu.make_async_remote_copy(
                src_ref=buf.at[tn], dst_ref=buf.at[tn],
                send_sem=v_ss.at[n, peer], recv_sem=v_rs.at[n, peer],
                device_id=ten_dev(peer), device_id_type=MESH,
            ).wait_send()
            return carry

        lax.fori_loop(1, NTEN, one, 0)

    chips = [lax.rem(x + d, 4) for d in range(4)]
    other = 1 - c
    HALF = CH // 2

    def gather_start(n, buf):
        for h in range(2):
            part = buf.at[tn, pl.ds(h * HALF, HALF)]
            for d in (2, 1, 3):
                send(part, part, ag_ss.at[n, d, h], ag_rs.at[n, d, h], ten_dev(chips[d] * 2 + c))
            send(part, part, sib_ss.at[n, 0, h], sib_rs.at[n, 0, h], ten_dev(x * 2 + other))

    def gather_forward(n, buf):
        for d in (1, 3, 2):
            src = lax.rem(x + 4 - d, 4) * 2 + c
            for h in range(2):
                part = buf.at[src, pl.ds(h * HALF, HALF)]
                wait_recv(part, ag_ss.at[n, d, h], ag_rs.at[n, d, h])
                send(part, part, sib_ss.at[n, d, h], sib_rs.at[n, d, h], ten_dev(x * 2 + other))

    def gather_chip(n, buf, d):
        chip = lax.rem(x + 4 - d, 4)
        for h in range(2):
            part = buf.at[chip * 2 + other, pl.ds(h * HALF, HALF)]
            wait_recv(part, sib_ss.at[n, d, h], sib_rs.at[n, d, h])
        return chip, buf[pl.ds(chip * 2, 2)].reshape(2 * CH, TOK)

    def gather_matmul(n, buf, weights):
        acc = None
        for d in (0, 1, 3, 2):
            chip, block = gather_chip(n, buf, d)
            term = mm(weights[chip], block)
            acc = term if acc is None else acc + term
        return acc

    def scatter_start(n, part_of, p, sb, q, t):
        for d in (2, 1, 3, 0):
            p[d] = part_of(chips[d] * 2 + other).astype(BF16)
            send(p.at[d], sb.at[d], rsib_ss.at[n, d], rsib_rs.at[n, d], ten_dev(x * 2 + other))
        for d in (2, 1, 3, 0):
            own[d] = part_of(chips[d] * 2 + c)
        for d in (2, 1, 3):
            wait_recv(sb.at[d], rsib_ss.at[n, d], rsib_rs.at[n, d])
            q[d] = (own[d] + sb[d].astype(F32)).astype(BF16)
            send(q.at[d], t.at[d], rs_ss.at[n, d], rs_rs.at[n, d], ten_dev(chips[d] * 2 + c))

    def scatter_end(n, sb, t):
        wait_recv(sb.at[0], rsib_ss.at[n, 0], rsib_rs.at[n, 0])
        total = own[0] + sb[0].astype(F32)
        for d in (1, 3, 2):
            wait_recv(t.at[d], rs_ss.at[n, d], rs_rs.at[n, d])
            total = total + t[d].astype(F32)
        return total

    r1[tn] = (res * gain).astype(BF16)
    gather_start(0, r1)
    share_row(0, v1, jnp.sum(res * res, axis=0, keepdims=True))
    gather_forward(0, r1)
    pre = gather_matmul(0, r1, wguT)
    inv = lax.rsqrt(sum_rows(0, v1) / D + EPS)
    gate_pre = pre[0:HID] * inv
    up_pre = pre[HID : 2 * HID] * inv
    sig = jax.nn.sigmoid(gate_pre)
    hidden = (gate_pre * sig * up_pre).astype(BF16)
    hid_s[...] = hidden
    gate_s[...] = gate_pre
    up_s[...] = up_pre

    scatter_start(0, lambda r: mm(wd[pl.ds(pl.multiple_of(r * CH, CH), CH), :], hid_s[...]), p1, sb1, q1, t1)
    projected = scatter_end(0, sb1, t1)
    summed = res_s[...] + projected
    cot = (summed - tgtT).astype(BF16)
    r2[tn] = cot
    gather_start(1, r2)
    out_ref[...] = mm(eye_t, summed.astype(BF16), 1, 1).astype(BF16)
    gather_forward(1, r2)
    d_hidden = gather_matmul(1, r2, wdT)

    gate_pre = gate_s[...]
    up_pre = up_s[...]
    sig = jax.nn.sigmoid(gate_pre)
    d_gate = (d_hidden * up_pre * sig * (1.0 + gate_pre * (1.0 - sig))).astype(BF16)
    d_up = (d_hidden * gate_pre * sig).astype(BF16)
    inner = d_gate.astype(F32) * gate_pre + d_up.astype(F32) * up_pre
    share_row(1, v2, jnp.sum(inner, axis=0, keepdims=True))

    def back_part(r):
        block = pl.ds(pl.multiple_of(r * CH, CH), CH)
        return mm(wg[block, :], d_gate) + mm(wu[block, :], d_up)

    scatter_start(1, back_part, p2, sb2, q2, t2)

    hid = hid_s[...]
    for r in range(NTEN):
        g = mm(r2[r], hid, 1, 1)
        zl, yhi = r // 2, r % 2
        for m in range(4):
            ya[yhi * 4 + m, zl * 48 : zl * 48 + 48, :] = g[m * 48 : m * 48 + 48, 0:GY].astype(BF16)
        for half in range(2):
            pieces = [g[m * 48 + half * 24 : m * 48 + half * 24 + 24, GY:HID] for m in range(4)]
            zb[half * 4 + zl, yhi * 96 : yhi * 96 + 96, :] = jnp.concatenate(pieces, axis=0).astype(BF16)

    def grad_send(n, src, dst, me, dev):
        def one(i, carry):
            peer = lax.rem(me + i, 8)
            pltpu.make_async_remote_copy(
                src_ref=src(peer), dst_ref=dst.at[me],
                send_sem=g_ss.at[n, peer], recv_sem=g_rs.at[n, me],
                device_id=dev(peer), device_id_type=MESH,
            ).start()
            return carry

        lax.fori_loop(1, 8, one, 0)

    def grad_sum(n, first, dst, me):
        def one(i, acc):
            peer = lax.rem(me + i, 8)
            wait_recv(dst.at[peer], g_ss.at[n, peer], g_rs.at[n, peer])
            return acc + dst[peer].astype(F32)

        return lax.fori_loop(1, 8, one, first)

    def grad_done(n, src, me, dev):
        def one(i, carry):
            peer = lax.rem(me + i, 8)
            pltpu.make_async_remote_copy(
                src_ref=src(peer), dst_ref=src(peer),
                send_sem=g_ss.at[n, peer], recv_sem=g_rs.at[n, peer],
                device_id=dev(peer), device_id_type=MESH,
            ).wait_send()
            return carry

        lax.fori_loop(1, 8, one, 0)

    def ya_of(yy):
        return ya.at[yy]

    def zb_of(zz):
        return zb.at[zz]

    def y2_of(zz):
        return y2s.at[pl.ds(pl.multiple_of(lax.rem(zz, 4) * 48 + (zz // 4) * 24, 8), ROWS)]

    def z2_of(yy):
        return z2s.at[pl.ds(pl.multiple_of(yy * ROWS, 8), ROWS)]

    grad_send(0, ya_of, yr, y, y_dev)
    grad_send(1, zb_of, zr, z, z_dev)

    d_normed = scatter_end(1, sb2, t2)
    corr = sum_rows(1, v2) / D
    res = res_s[...]
    d_res = (cot.astype(F32) + inv * (gain * d_normed - res * inv * corr)).astype(BF16)
    d_tok = mm(eye_t, d_res, 1, 1)
    a3s[...] = d_tok.astype(BF16).reshape(NSEQ, POS, CH)

    all_to_all_send(2, a3s, a3r)
    all_to_all_wait(2, a3s, a3r)
    weighted = (a3r[...].reshape(TOK, CH).astype(F32) * tout).astype(BF16)
    a4s[...] = mm(kronT[...], weighted).astype(BF16).reshape(NSEQ, POS, CH)
    all_to_all_send(3, a4s, a4r)

    y2s[...] = grad_sum(0, ya[y].astype(F32), yr, y)
    grad_send(2, y2_of, y2r, z, z_dev)
    z2s[...] = grad_sum(1, zb[z].astype(F32), zr, z)
    grad_send(3, z2_of, z2r, y, y_dev)

    all_to_all_wait(3, a4s, a4r)
    scaled = (a4r[...].reshape(TOK, CH).astype(F32) * tin).astype(BF16)
    d_mix = mm(bm_ref[...], scaled)
    din_ref[...] = (a3s[...].reshape(TOK, CH).astype(F32) + d_mix).astype(BF16)

    gd_ref[:, 0:GY] = grad_sum(2, y2s[pl.ds(pl.multiple_of(dp * 48 + zh * 24, 8), ROWS), :], y2r, z)
    gd_ref[:, GY:HID] = grad_sum(3, z2s[pl.ds(pl.multiple_of(y * ROWS, 8), ROWS), :], z2r, y)

    for cp in sent:
        cp.wait_send()
    for n, src in enumerate((a1s, a2s, a3s, a4s)):
        all_to_all_done(n, src)
    rows_done(0, v1)
    rows_done(1, v2)
    grad_done(0, ya_of, y, y_dev)
    grad_done(1, zb_of, z, z_dev)
    grad_done(2, y2_of, z, z_dev)
    grad_done(3, z2_of, y, y_dev)


def body(
    inputs, targets, block_mix, cross_mix, twiddle_in, twiddle_out, norm_gain, w_gate, w_up, w_down
):
    vmem = pl.BlockSpec(memory_space=pltpu.VMEM)
    hbm = pl.BlockSpec(memory_space=pl.ANY)
    dma = pltpu.SemaphoreType.DMA
    chunks = pltpu.VMEM((NSEQ, POS, CH), BF16)
    blocks4 = pltpu.VMEM((4, CH, TOK), BF16)
    output, d_input, grad_down = pl.pallas_call(
        kernel,
        out_shape=(
            jax.ShapeDtypeStruct((TOK, CH), BF16),
            jax.ShapeDtypeStruct((TOK, CH), BF16),
            jax.ShapeDtypeStruct((ROWS, HID), F32),
        ),
        in_specs=[vmem] * 7 + [hbm] * 3,
        out_specs=(vmem, vmem, vmem),
        scratch_shapes=[
            pltpu.VMEM((D, HID), BF16),
            pltpu.VMEM((D, HID), BF16),
            pltpu.VMEM((D, HID), BF16),
            pltpu.VMEM((4, 2 * HID, HID), BF16),
            pltpu.VMEM((4, HID, HID), BF16),
            pltpu.VMEM((TOK, TOK), BF16),
            pltpu.VMEM((TOK, TOK), BF16),
        ]
        + [chunks] * 8
        + [
            pltpu.VMEM((NTEN, CH, TOK), BF16),
            pltpu.VMEM((NTEN, CH, TOK), BF16),
            pltpu.VMEM((NTEN, 8, TOK), F32),
            pltpu.VMEM((NTEN, 8, TOK), F32),
        ]
        + [blocks4] * 8
        + [
            pltpu.VMEM((4, CH, TOK), F32),
            pltpu.VMEM((HID, TOK), F32),
            pltpu.VMEM((HID, TOK), F32),
            pltpu.VMEM((HID, TOK), BF16),
            pltpu.VMEM((CH, TOK), F32),
            pltpu.VMEM((8, CH, GY), BF16),
            pltpu.VMEM((8, CH, GY), BF16),
            pltpu.VMEM((8, CH, GZ), BF16),
            pltpu.VMEM((8, CH, GZ), BF16),
            pltpu.VMEM((CH, GY), F32),
            pltpu.VMEM((8, ROWS, GY), F32),
            pltpu.VMEM((CH, GZ), F32),
            pltpu.VMEM((8, ROWS, GZ), F32),
            dma((3,)),
            dma((4, NSEQ)),
            dma((4, NSEQ)),
            dma((2, 4, 2)),
            dma((2, 4, 2)),
            dma((2, 4, 2)),
            dma((2, 4, 2)),
            dma((2, NTEN)),
            dma((2, NTEN)),
            dma((2, 4)),
            dma((2, 4)),
            dma((2, 4)),
            dma((2, 4)),
            dma((4, 8)),
            dma((4, 8)),
        ],
        compiler_params=pltpu.CompilerParams(
            collective_id=0, has_side_effects=True, vmem_limit_bytes=48 * 1024 * 1024
        ),
        name="monarch_block",
    )(
        inputs[0],
        targets[0],
        block_mix,
        cross_mix,
        twiddle_in,
        twiddle_out,
        norm_gain.reshape(1, D),
        w_gate,
        w_up,
        w_down,
    )
    return output[None], d_input[None], grad_down


def solution(mesh):
    return jax.shard_map(
        body,
        mesh=mesh,
        in_specs=(
            P("dp", "seq", "tensor"),
            P("dp", "seq", "tensor"),
            P(),
            P(),
            P("seq", None),
            P(None, "seq"),
            P(),
            P(None, "tensor"),
            P(None, "tensor"),
            P(None, "tensor"),
        ),
        out_specs=(P("dp", "seq", "tensor"), P("dp", "seq", "tensor"), P(("dp", "seq"), "tensor")),
        check_vma=False,
    )
```

time: 550 us -> 112 us (0.20)
  the two profiles are of different devices: /device:TPU:92 before, /device:TPU:1 now
where the time goes in v1:
time: 112 us
  Pallas kernels  99.4 us (89%)
  local copies, waits for them, and re-layouts  11.6 us (10%)
    pallas_call x1, Pallas kernels, body(): pl.pallas_call(kernel, out_shape=(jax.ShapeDtypeStruct((TOK, CH), BF16),...  99.4 us
    unnamed x19, local copies, waits for them, and re-layouts  10.9 us

profile of v1, /device:TPU:1, one launch (start us, length us, event | category | flops | bytes accessed | tf_op | source)
XLA Modules:
  0.0 111.6 jit_solution(12067578941834064792)
XLA Ops:
  0.6 0.7 reshape.9.gain_ref
  1.3 1.0 copy.13
  2.3 1.0 copy.14
  3.3 0.0 copy-start
  3.3 1.3 %copy-done = bf16[1536,384]{1,0:T(8,128)(2,1)S(1)} copy-done((bf16[1536,384]{1,0:T(8,128)(2,1)S(1)}, bf16[1536,384]{1,0:T(8,128)(2,1)}, u32[]{:S(2)}) %copy-start) | copy-done | bytes 1179672
  4.6 0.0 copy-start.1
  4.6 1.3 %copy-done.1 = bf16[1536,384]{1,0:T(8,128)(2,1)S(1)} copy-done((bf16[1536,384]{1,0:T(8,128)(2,1)S(1)}, bf16[1536,384]{1,0:T(8,128)(2,1)}, u32[]{:S(2)}) %copy-start.1) | copy-done | bytes 1179672
  5.9 0.0 copy-start.2
  5.9 1.3 %copy-done.2 = bf16[1536,384]{1,0:T(8,128)(2,1)S(1)} copy-done((bf16[1536,384]{1,0:T(8,128)(2,1)S(1)}, bf16[1536,384]{1,0:T(8,128)(2,1)}, u32[]{:S(2)}) %copy-start.2) | copy-done | bytes 1179672
  7.1 0.0 copy-start.3
  7.1 0.9 copy-done.3
  8.0 0.0 copy-start.4
  8.1 0.7 copy-done.4
  8.7 0.0 copy-start.5
  8.7 0.7 copy-done.5
  9.4 0.0 copy-start.6
  9.4 0.7 copy-done.6
  10.1 99.4 %monarch_block.1 = (bf16[256,192]{1,0:T(8,128)(2,1)S(1)}, bf16[256,192]{1,0:T(8,128)(2,1)S(1)}, f32[24,384]{1,0:T(8,128)S(1)}) custom-call(bf16[256,192]{1,0:T(8,128)(2,1)S(1)} %bitcast.4, bf16[256,192]{1,0:T(8,128)(2,1)S(1)} %bitcast.5, bf16[256,256]{1,0:T(8,128)(2,1)S(1)} %copy-done.3, bf16[16,16]{1,0:T(8,128)(2,1)S(1)} %copy-done.5, ...), custom_call_target="tpu_custom_call" | custom-call | tf_op jit(solution)/shard_map/monarch_block/pallas_call | solution.py:424
  109.5 0.7 copy.15
  110.3 0.7 copy.16
  111.0 0.6 copy.18
Async XLA Ops:
  3.3 1.3 %copy-start = (bf16[1536,384]{1,0:T(8,128)(2,1)S(1)}, bf16[1536,384]{1,0:T(8,128)(2,1)}, u32[]{:S(2)}) copy-start(bf16[1536,384]{1,0:T(8,128)(2,1)} %wg_hbm.1) | copy-start | bytes 3538948
  4.6 1.3 %copy-start.1 = (bf16[1536,384]{1,0:T(8,128)(2,1)S(1)}, bf16[1536,384]{1,0:T(8,128)(2,1)}, u32[]{:S(2)}) copy-start(bf16[1536,384]{1,0:T(8,128)(2,1)} %wu_hbm.1) | copy-start | bytes 3538948
  5.9 1.3 %copy-start.2 = (bf16[1536,384]{1,0:T(8,128)(2,1)S(1)}, bf16[1536,384]{1,0:T(8,128)(2,1)}, u32[]{:S(2)}) copy-start(bf16[1536,384]{1,0:T(8,128)(2,1)} %wd_hbm.1) | copy-start | bytes 3538948
  7.1 0.9 copy-start.3
  8.0 0.7 copy-start.4
  8.7 0.7 copy-start.5
  9.4 0.7 copy-start.6

commit v2 on v1

--- a/solution.py
+++ b/solution.py
@@ -18,8 +18,7 @@
 NTEN = 8
 POS = 16
 D = 1536
-GY = 256
-GZ = HID - GY
+LANES = 128
 ROWS = 24
 EPS = 1e-05
 
@@ -40,15 +39,16 @@
 
 
 def kernel(
-    x_ref, tgt_ref, bm_ref, cm_ref, ti_ref, to_ref, gain_ref, wg_hbm, wu_hbm, wd_hbm,
-    out_ref, din_ref, gd_ref,
+    x_hbm, tgt_hbm, bm_hbm, cm_hbm, ti_hbm, to_hbm, gain_hbm, wg_hbm, wu_hbm, wd_hbm,
+    out_hbm, din_hbm, gd_hbm,
+    out_ref, din_ref, gd_ref, x_ref, tgt_ref, bm_ref, cm_ref, ti_ref, to_ref, gain_ref,
     wg, wu, wd, wguT, wdT, kron, kronT,
     a1s, a1r, a2s, a2r, a3s, a3r, a4s, a4r,
     r1, r2, v1, v2,
     p1, p2, sb1, sb2, q1, q2, t1, t2, own, gate_s, up_s, hid_s, res_s,
     ya, yr, zb, zr, y2s, y2r, z2s, z2r,
-    wsem, a_ss, a_rs, ag_ss, ag_rs, sib_ss, sib_rs, v_ss, v_rs,
-    rsib_ss, rsib_rs, rs_ss, rs_rs, g_ss, g_rs,
+    osem, wsem, a_ss, a_rs, ag_ss, ag_rs, sib_ss, sib_rs, v_ss, v_rs,
+    rsib_ss, rsib_rs, rs_ss, rs_rs, gy_ss, gy_rs, gz_ss, gz_rs, g2_ss, g2_rs,
 ):
     dp = lax.axis_index("dp")
     sq = lax.axis_index("seq")
@@ -69,14 +69,19 @@
     def z_dev(zz):
         return (lax.rem(zz, 4), y * 2 + zz // 4, tn)
 
-    sent = []
+    pending = []
+
+    def drain():
+        while pending:
+            pending.pop(0)()
+
 
     def send(src, dst, ss, rs, dev):
         cp = pltpu.make_async_remote_copy(
             src_ref=src, dst_ref=dst, send_sem=ss, recv_sem=rs, device_id=dev, device_id_type=MESH
         )
         cp.start()
-        sent.append(cp)
+        pending.append(cp.wait_send)
 
     def wait_recv(buf, ss, rs):
         pltpu.make_async_remote_copy(
@@ -84,6 +89,18 @@
             device_id=(dp, sq, tn), device_id_type=MESH,
         ).wait_recv()
 
+    loads = []
+    for n, (src, dst) in enumerate(
+        (
+            (x_hbm, x_ref), (bm_hbm, bm_ref), (ti_hbm, ti_ref), (cm_hbm, cm_ref), (to_hbm, to_ref),
+            (gain_hbm, gain_ref), (wg_hbm, wg), (wu_hbm, wu), (wd_hbm, wd), (tgt_hbm, tgt_ref),
+        )
+    ):
+        cp = pltpu.make_async_copy(src, dst, wsem.at[n])
+        loads.append(cp)
+    for cp in loads[0:3]:
+        cp.start()
+
     barrier = pltpu.get_barrier_semaphore()
 
     def greet(dev):
@@ -102,11 +119,13 @@
     for i in (1, 2, 3, 5, 6, 7):
         greet(z_dev(lax.rem(z + i, 8)))
 
-    loads = []
-    for n, (src, dst) in enumerate(((wg_hbm, wg), (wu_hbm, wu), (wd_hbm, wd))):
-        cp = pltpu.make_async_copy(src, dst, wsem.at[n])
+    for cp in loads[3:]:
         cp.start()
-        loads.append(cp)
+
+    def store(n, src, dst):
+        cp = pltpu.make_async_copy(src, dst, osem.at[n])
+        cp.start()
+        pending.append(cp.wait)
 
     def all_to_all_send(n, src, dst):
         def one(i, carry):
@@ -120,6 +139,7 @@
 
         lax.fori_loop(1, NSEQ, one, 0)
         dst[sq] = src[sq]
+        pending.append(functools.partial(all_to_all_done, n, src))
 
     def all_to_all_wait(n, src, dst):
         def one(i, carry):
@@ -141,8 +161,10 @@
 
         lax.fori_loop(1, NSEQ, one, 0)
 
+    for cp in loads[0:3]:
+        cp.wait()
     tin = column_of(ti_ref[...])
-    section = mm(bm_ref[...], x_ref[...], 0, 0) * tin
+    section = mm(bm_ref[...], x_ref[...], 0, 1) * tin
     a1s[...] = section.astype(BF16).reshape(NSEQ, POS, CH)
 
     pl.semaphore_wait(barrier, (NSEQ - 1) + (NTEN - 1) + 6)
@@ -152,6 +174,8 @@
     cols = lax.broadcasted_iota(jnp.int32, (TOK, NSEQ), 1)
     pick_block = jnp.where(rows // POS == cols, 1.0, 0.0)
     pick_pos = jnp.where(rows % POS == cols, 1.0, 0.0)
+    for cp in loads[3:6]:
+        cp.wait()
     cross = cm_ref[...]
     wide = mm(pick_block.astype(BF16), cross, 1, 1).astype(BF16)
     wide = mm(wide, pick_block.astype(BF16), 1, 1)
@@ -164,12 +188,13 @@
     kronT[...] = jnp.where(same_pos, wideT, 0.0).astype(BF16)
     tout_all = jnp.broadcast_to(to_ref[...][:, None, :], (NSEQ, POS, POS)).reshape(TOK, POS)
     tout = jnp.sum(tout_all * pick_pos, axis=1, keepdims=True)
-    gains = gain_ref[...]
-    gain_row = jnp.zeros((1, CH), F32)
-    for r in range(NTEN):
-        gain_row = gain_row + jnp.where(tn == r, gains[:, r * CH : (r + 1) * CH], 0.0)
-    gain = column_of(gain_row)
-    for cp in loads:
+    flat = tn * CH + lax.broadcasted_iota(jnp.int32, (CH, 128), 0)
+    lane = lax.broadcasted_iota(jnp.int32, (CH, 128), 1)
+    gain = jnp.zeros((CH, 128), F32)
+    for k in range(D // 128):
+        gain = gain + jnp.where(flat == k * 128 + lane, gain_ref[k : k + 1, :], 0.0)
+    gain = jnp.sum(gain, axis=1, keepdims=True)
+    for cp in loads[6:]:
         cp.wait()
     eye_h = eye(HID)
     for k in range(4):
@@ -179,7 +204,6 @@
         wdT[k] = mm(eye_h, wd[block, :], 1, 1).astype(BF16)
     eye_c = eye(CH)
     eye_t = eye(TOK)
-    tgtT = mm(eye_c, tgt_ref[...], 1, 1)
 
     all_to_all_wait(0, a1s, a1r)
 
@@ -188,8 +212,8 @@
     all_to_all_send(1, a2s, a2r)
     all_to_all_wait(1, a2s, a2r)
 
-    residual = (x_ref[...].astype(F32) + a2r[...].reshape(TOK, CH).astype(F32)).astype(BF16)
-    res = mm(eye_c, residual, 1, 1)
+    mixed = mm(eye_c, a2r[...].reshape(TOK, CH), 1, 1)
+    res = (x_ref[...].astype(F32) + mixed).astype(BF16).astype(F32)
     res_s[...] = res
 
     def share_row(n, buf, row):
@@ -205,6 +229,7 @@
             return carry
 
         lax.fori_loop(1, NTEN, one, 0)
+        pending.append(functools.partial(rows_done, n, buf))
 
     def sum_rows(n, buf):
         def one(i, carry):
@@ -238,13 +263,15 @@
                 send(part, part, ag_ss.at[n, d, h], ag_rs.at[n, d, h], ten_dev(chips[d] * 2 + c))
             send(part, part, sib_ss.at[n, 0, h], sib_rs.at[n, 0, h], ten_dev(x * 2 + other))
 
-    def gather_forward(n, buf):
+    def gather_forward(n, buf, then=None):
         for d in (1, 3, 2):
             src = lax.rem(x + 4 - d, 4) * 2 + c
             for h in range(2):
                 part = buf.at[src, pl.ds(h * HALF, HALF)]
                 wait_recv(part, ag_ss.at[n, d, h], ag_rs.at[n, d, h])
                 send(part, part, sib_ss.at[n, d, h], sib_rs.at[n, d, h], ten_dev(x * 2 + other))
+            if then is not None:
+                then(src // 2, c)
 
     def gather_chip(n, buf, d):
         chip = lax.rem(x + 4 - d, 4)
@@ -253,20 +280,21 @@
             wait_recv(part, sib_ss.at[n, d, h], sib_rs.at[n, d, h])
         return chip, buf[pl.ds(chip * 2, 2)].reshape(2 * CH, TOK)
 
-    def gather_matmul(n, buf, weights):
-        acc = None
-        for d in (0, 1, 3, 2):
+    def gather_matmul(n, buf, weights, offsets, acc=None):
+        for d in offsets:
             chip, block = gather_chip(n, buf, d)
             term = mm(weights[chip], block)
             acc = term if acc is None else acc + term
         return acc
 
-    def scatter_start(n, part_of, p, sb, q, t):
+    def scatter_start(n, part_of, p, sb, q, t, then=None):
         for d in (2, 1, 3, 0):
             p[d] = part_of(chips[d] * 2 + other).astype(BF16)
             send(p.at[d], sb.at[d], rsib_ss.at[n, d], rsib_rs.at[n, d], ten_dev(x * 2 + other))
         for d in (2, 1, 3, 0):
             own[d] = part_of(chips[d] * 2 + c)
+        if then is not None:
+            then()
         for d in (2, 1, 3):
             wait_recv(sb.at[d], rsib_ss.at[n, d], rsib_rs.at[n, d])
             q[d] = (own[d] + sb[d].astype(F32)).astype(BF16)
@@ -283,8 +311,9 @@
     r1[tn] = (res * gain).astype(BF16)
     gather_start(0, r1)
     share_row(0, v1, jnp.sum(res * res, axis=0, keepdims=True))
+    pre = gather_matmul(0, r1, wguT, (0,))
     gather_forward(0, r1)
-    pre = gather_matmul(0, r1, wguT)
+    pre = gather_matmul(0, r1, wguT, (1, 3, 2), pre)
     inv = lax.rsqrt(sum_rows(0, v1) / D + EPS)
     gate_pre = pre[0:HID] * inv
     up_pre = pre[HID : 2 * HID] * inv
@@ -294,15 +323,167 @@
     gate_s[...] = gate_pre
     up_s[...] = up_pre
 
+    def grad_rank(chip, yhi):
+        g = mm(r2[chip * 2 + yhi], hid_s[...], 1, 1)
+        first, second, third = (g[:, n * LANES : (n + 1) * LANES] for n in range(3))
+        for m in range(4):
+            ya[chip, yhi * 4 + m, 0:48, :] = first[m * 48 : m * 48 + 48].astype(BF16)
+            ya[chip, yhi * 4 + m, 48:96, :] = third[m * 48 : m * 48 + 48].astype(BF16)
+        for half in range(2):
+            for at, part in ((0, second), (96, third)):
+                pieces = [part[m * 48 + half * ROWS : m * 48 + half * ROWS + ROWS] for m in range(4)]
+                zb[half * 4 + chip, yhi, at : at + 96, :] = jnp.concatenate(pieces, axis=0).astype(BF16)
+
+        def send_all(y_rows, z_rows):
+            for m in range(4):
+                peer = yhi * 4 + m
+
+                @pl.when(peer != y)
+                def _():
+                    pltpu.make_async_remote_copy(
+                        src_ref=ya.at[chip, peer, pl.ds(0, y_rows)],
+                        dst_ref=yr.at[chip, y, pl.ds(0, y_rows)],
+                        send_sem=gy_ss.at[chip, peer], recv_sem=gy_rs.at[chip, y],
+                        device_id=y_dev(peer), device_id_type=MESH,
+                    ).start()
+
+            for half in range(2):
+                zpeer = half * 4 + chip
+
+                @pl.when(zpeer != z)
+                def _():
+                    pltpu.make_async_remote_copy(
+                        src_ref=zb.at[zpeer, yhi, pl.ds(0, z_rows)],
+                        dst_ref=zr.at[z, yhi, pl.ds(0, z_rows)],
+                        send_sem=gz_ss.at[zpeer, yhi], recv_sem=gz_rs.at[z, yhi],
+                        device_id=z_dev(zpeer), device_id_type=MESH,
+                    ).start()
+
+        @pl.when(chip < 2)
+        def _():
+            send_all(96, 96)
+
+        @pl.when(chip >= 2)
+        def _():
+            send_all(48, 2 * 96)
+
+    def grad_first_done():
+        def one(i, carry):
+            peer = lax.rem(y + i, 8)
+            for zl in range(4):
+                buf = ya.at[zl, peer, pl.ds(0, 96 if zl < 2 else 48)]
+                pltpu.make_async_remote_copy(
+                    src_ref=buf, dst_ref=buf, send_sem=gy_ss.at[zl, peer], recv_sem=gy_rs.at[zl, peer],
+                    device_id=y_dev(peer), device_id_type=MESH,
+                ).wait_send()
+            return carry
+
+        lax.fori_loop(1, 8, one, 0)
+        for zz in range(8):
+
+            @pl.when(z != zz)
+            def _():
+                for yhi in range(2):
+                    buf = zb.at[zz, yhi, pl.ds(0, 96 if zz % 4 < 2 else 2 * 96)]
+                    pltpu.make_async_remote_copy(
+                        src_ref=buf, dst_ref=buf, send_sem=gz_ss.at[zz, yhi],
+                        recv_sem=gz_rs.at[zz, yhi], device_id=z_dev(zz), device_id_type=MESH,
+                    ).wait_send()
+
+    def grad_second():
+        for zl in range(4):
+            rows = 96 if zl < 2 else 48
+
+            def add(i, acc):
+                peer = lax.rem(y + i, 8)
+                buf = yr.at[zl, peer, pl.ds(0, rows)]
+                wait_recv(buf, gy_ss.at[zl, peer], gy_rs.at[zl, peer])
+                return acc + buf[...].astype(F32)
+
+            total = lax.fori_loop(1, 8, add, ya[zl, y, 0:rows, :].astype(F32))
+            for half in range(2):
+                pieces = [total[half * ROWS : half * ROWS + ROWS]]
+                if zl < 2:
+                    pieces.append(total[48 + half * ROWS : 48 + half * ROWS + ROWS])
+                else:
+                    pieces.append(jnp.zeros((ROWS, LANES), F32))
+                y2s[half * 4 + zl] = jnp.concatenate(pieces, axis=0).astype(BF16)
+        second_send(0, y2s, y2r, z, z_dev)
+
+        def sum_z(rows):
+            for yhi in range(2):
+
+                def add(i, acc):
+                    peer = lax.rem(z + i, 8)
+                    buf = zr.at[peer, yhi, pl.ds(0, rows)]
+                    wait_recv(buf, gz_ss.at[peer, yhi], gz_rs.at[peer, yhi])
+                    return acc + buf[...].astype(F32)
+
+                total = lax.fori_loop(1, 8, add, zb[z, yhi, 0:rows, :].astype(F32))
+                for m in range(4):
+                    pieces = [total[m * ROWS : m * ROWS + ROWS]]
+                    if rows > 96:
+                        pieces.append(total[96 + m * ROWS : 96 + m * ROWS + ROWS])
+                    else:
+                        pieces.append(jnp.zeros((ROWS, LANES), F32))
+                    z2s[yhi * 4 + m] = jnp.concatenate(pieces, axis=0).astype(BF16)
+
+        @pl.when(dp < 2)
+        def _():
+            sum_z(96)
+
+        @pl.when(dp >= 2)
+        def _():
+            sum_z(2 * 96)
+
+        second_send(1, z2s, z2r, y, y_dev)
+
+    def second_send(n, src, dst, me, dev):
+        def one(i, carry):
+            peer = lax.rem(me + i, 8)
+            pltpu.make_async_remote_copy(
+                src_ref=src.at[peer], dst_ref=dst.at[me],
+                send_sem=g2_ss.at[n, peer], recv_sem=g2_rs.at[n, me],
+                device_id=dev(peer), device_id_type=MESH,
+            ).start()
+            return carry
+
+        lax.fori_loop(1, 8, one, 0)
+        pending.append(functools.partial(second_done, n, src, me, dev))
+
+    def second_done(n, src, me, dev):
+        def one(i, carry):
+            peer = lax.rem(me + i, 8)
+            pltpu.make_async_remote_copy(
+                src_ref=src.at[peer], dst_ref=src.at[peer],
+                send_sem=g2_ss.at[n, peer], recv_sem=g2_rs.at[n, peer],
+                device_id=dev(peer), device_id_type=MESH,
+            ).wait_send()
+            return carry
+
+        lax.fori_loop(1, 8, one, 0)
+
+    def second_sum(n, src, dst, me):
+        def add(i, acc):
+            peer = lax.rem(me + i, 8)
+            wait_recv(dst.at[peer], g2_ss.at[n, peer], g2_rs.at[n, peer])
+            return acc + dst[peer].astype(F32)
+
+        return lax.fori_loop(1, 8, add, src[me].astype(F32))
+
     scatter_start(0, lambda r: mm(wd[pl.ds(pl.multiple_of(r * CH, CH), CH), :], hid_s[...]), p1, sb1, q1, t1)
     projected = scatter_end(0, sb1, t1)
     summed = res_s[...] + projected
-    cot = (summed - tgtT).astype(BF16)
+    cot = (summed - tgt_ref[...].astype(F32)).astype(BF16)
     r2[tn] = cot
     gather_start(1, r2)
-    out_ref[...] = mm(eye_t, summed.astype(BF16), 1, 1).astype(BF16)
-    gather_forward(1, r2)
-    d_hidden = gather_matmul(1, r2, wdT)
+    out_ref[...] = summed.astype(BF16)
+    store(0, out_ref, out_hbm)
+    grad_rank(x, c)
+    d_hidden = gather_matmul(1, r2, wdT, (0,))
+    grad_rank(x, other)
+    gather_forward(1, r2, grad_rank)
+    d_hidden = gather_matmul(1, r2, wdT, (1, 3, 2), d_hidden)
 
     gate_pre = gate_s[...]
     up_pre = up_s[...]
@@ -316,64 +497,12 @@
         block = pl.ds(pl.multiple_of(r * CH, CH), CH)
         return mm(wg[block, :], d_gate) + mm(wu[block, :], d_up)
 
-    scatter_start(1, back_part, p2, sb2, q2, t2)
-
-    hid = hid_s[...]
-    for r in range(NTEN):
-        g = mm(r2[r], hid, 1, 1)
-        zl, yhi = r // 2, r % 2
-        for m in range(4):
-            ya[yhi * 4 + m, zl * 48 : zl * 48 + 48, :] = g[m * 48 : m * 48 + 48, 0:GY].astype(BF16)
-        for half in range(2):
-            pieces = [g[m * 48 + half * 24 : m * 48 + half * 24 + 24, GY:HID] for m in range(4)]
-            zb[half * 4 + zl, yhi * 96 : yhi * 96 + 96, :] = jnp.concatenate(pieces, axis=0).astype(BF16)
-
-    def grad_send(n, src, dst, me, dev):
-        def one(i, carry):
-            peer = lax.rem(me + i, 8)
-            pltpu.make_async_remote_copy(
-                src_ref=src(peer), dst_ref=dst.at[me],
-                send_sem=g_ss.at[n, peer], recv_sem=g_rs.at[n, me],
-                device_id=dev(peer), device_id_type=MESH,
-            ).start()
-            return carry
-
-        lax.fori_loop(1, 8, one, 0)
-
-    def grad_sum(n, first, dst, me):
-        def one(i, acc):
-            peer = lax.rem(me + i, 8)
-            wait_recv(dst.at[peer], g_ss.at[n, peer], g_rs.at[n, peer])
-            return acc + dst[peer].astype(F32)
-
-        return lax.fori_loop(1, 8, one, first)
-
-    def grad_done(n, src, me, dev):
-        def one(i, carry):
-            peer = lax.rem(me + i, 8)
-            pltpu.make_async_remote_copy(
-                src_ref=src(peer), dst_ref=src(peer),
-                send_sem=g_ss.at[n, peer], recv_sem=g_rs.at[n, peer],
-                device_id=dev(peer), device_id_type=MESH,
-            ).wait_send()
-            return carry
-
-        lax.fori_loop(1, 8, one, 0)
-
-    def ya_of(yy):
-        return ya.at[yy]
-
-    def zb_of(zz):
-        return zb.at[zz]
-
-    def y2_of(zz):
-        return y2s.at[pl.ds(pl.multiple_of(lax.rem(zz, 4) * 48 + (zz // 4) * 24, 8), ROWS)]
-
-    def z2_of(yy):
-        return z2s.at[pl.ds(pl.multiple_of(yy * ROWS, 8), ROWS)]
-
-    grad_send(0, ya_of, yr, y, y_dev)
-    grad_send(1, zb_of, zr, z, z_dev)
+    def grad_rest():
+        for d in (1, 3, 2):
+            grad_rank(chips[d], other)
+        pending.append(grad_first_done)
+
+    scatter_start(1, back_part, p2, sb2, q2, t2, grad_rest)
 
     d_normed = scatter_end(1, sb2, t2)
     corr = sum_rows(1, v2) / D
@@ -383,54 +512,65 @@
     a3s[...] = d_tok.astype(BF16).reshape(NSEQ, POS, CH)
 
     all_to_all_send(2, a3s, a3r)
+    grad_second()
     all_to_all_wait(2, a3s, a3r)
     weighted = (a3r[...].reshape(TOK, CH).astype(F32) * tout).astype(BF16)
     a4s[...] = mm(kronT[...], weighted).astype(BF16).reshape(NSEQ, POS, CH)
     all_to_all_send(3, a4s, a4r)
 
-    y2s[...] = grad_sum(0, ya[y].astype(F32), yr, y)
-    grad_send(2, y2_of, y2r, z, z_dev)
-    z2s[...] = grad_sum(1, zb[z].astype(F32), zr, z)
-    grad_send(3, z2_of, z2r, y, y_dev)
-
+    rows_y = second_sum(0, y2s, y2r, z)
+    rows_z = second_sum(1, z2s, z2r, y)
+    gd_ref[:, 0:LANES] = rows_y[0:ROWS]
+    gd_ref[:, LANES : 2 * LANES] = rows_z[0:ROWS]
+    gd_ref[:, 2 * LANES : HID] = rows_y[ROWS:48] + rows_z[ROWS:48]
+    store(2, gd_ref, gd_hbm)
+
+    drain()
     all_to_all_wait(3, a4s, a4r)
     scaled = (a4r[...].reshape(TOK, CH).astype(F32) * tin).astype(BF16)
-    d_mix = mm(bm_ref[...], scaled)
-    din_ref[...] = (a3s[...].reshape(TOK, CH).astype(F32) + d_mix).astype(BF16)
-
-    gd_ref[:, 0:GY] = grad_sum(2, y2s[pl.ds(pl.multiple_of(dp * 48 + zh * 24, 8), ROWS), :], y2r, z)
-    gd_ref[:, GY:HID] = grad_sum(3, z2s[pl.ds(pl.multiple_of(y * ROWS, 8), ROWS), :], z2r, y)
-
-    for cp in sent:
-        cp.wait_send()
-    for n, src in enumerate((a1s, a2s, a3s, a4s)):
-        all_to_all_done(n, src)
-    rows_done(0, v1)
-    rows_done(1, v2)
-    grad_done(0, ya_of, y, y_dev)
-    grad_done(1, zb_of, z, z_dev)
-    grad_done(2, y2_of, z, z_dev)
-    grad_done(3, z2_of, y, y_dev)
+    d_mix = mm(scaled, bm_ref[...], 0, 1)
+    din_ref[...] = (d_res.astype(F32) + d_mix).astype(BF16)
+
+    store(1, din_ref, din_hbm)
+
+    drain()
+
+
+def finish(out_in, din_in, gd_in, out_ref, din_ref, gd_ref):
+    out_ref[...] = out_in[...]
+    din_ref[...] = din_in[...]
+    gd_ref[...] = gd_in[...]
 
 
 def body(
     inputs, targets, block_mix, cross_mix, twiddle_in, twiddle_out, norm_gain, w_gate, w_up, w_down
 ):
+    hbm = pl.BlockSpec(memory_space=pltpu.HBM)
     vmem = pl.BlockSpec(memory_space=pltpu.VMEM)
-    hbm = pl.BlockSpec(memory_space=pl.ANY)
     dma = pltpu.SemaphoreType.DMA
     chunks = pltpu.VMEM((NSEQ, POS, CH), BF16)
     blocks4 = pltpu.VMEM((4, CH, TOK), BF16)
-    output, d_input, grad_down = pl.pallas_call(
+    results = (
+        jax.ShapeDtypeStruct((CH, TOK), BF16),
+        jax.ShapeDtypeStruct((CH, TOK), BF16),
+        jax.ShapeDtypeStruct((ROWS, HID), F32),
+    )
+    made = pl.pallas_call(
         kernel,
-        out_shape=(
-            jax.ShapeDtypeStruct((TOK, CH), BF16),
-            jax.ShapeDtypeStruct((TOK, CH), BF16),
-            jax.ShapeDtypeStruct((ROWS, HID), F32),
-        ),
-        in_specs=[vmem] * 7 + [hbm] * 3,
-        out_specs=(vmem, vmem, vmem),
+        out_shape=results,
+        in_specs=[hbm] * 10,
+        out_specs=(hbm, hbm, hbm),
         scratch_shapes=[
+            pltpu.VMEM((CH, TOK), BF16),
+            pltpu.VMEM((CH, TOK), BF16),
+            pltpu.VMEM((ROWS, HID), F32),
+            pltpu.VMEM((CH, TOK), BF16),
+            pltpu.VMEM((CH, TOK), BF16),
+            pltpu.VMEM((TOK, TOK), BF16),
+            pltpu.VMEM((NSEQ, NSEQ), BF16),
+            pltpu.VMEM((1, TOK), F32),
+            pltpu.VMEM((NSEQ, POS), F32),
+            pltpu.VMEM((D // 128, 128), F32),
             pltpu.VMEM((D, HID), BF16),
             pltpu.VMEM((D, HID), BF16),
             pltpu.VMEM((D, HID), BF16),
@@ -453,15 +593,16 @@
             pltpu.VMEM((HID, TOK), F32),
             pltpu.VMEM((HID, TOK), BF16),
             pltpu.VMEM((CH, TOK), F32),
-            pltpu.VMEM((8, CH, GY), BF16),
-            pltpu.VMEM((8, CH, GY), BF16),
-            pltpu.VMEM((8, CH, GZ), BF16),
-            pltpu.VMEM((8, CH, GZ), BF16),
-            pltpu.VMEM((CH, GY), F32),
-            pltpu.VMEM((8, ROWS, GY), F32),
-            pltpu.VMEM((CH, GZ), F32),
-            pltpu.VMEM((8, ROWS, GZ), F32),
+            pltpu.VMEM((4, 8, 96, LANES), BF16),
+            pltpu.VMEM((4, 8, 96, LANES), BF16),
+            pltpu.VMEM((8, 2, 2 * 96, LANES), BF16),
+            pltpu.VMEM((8, 2, 2 * 96, LANES), BF16),
+            pltpu.VMEM((8, 48, LANES), BF16),
+            pltpu.VMEM((8, 48, LANES), BF16),
+            pltpu.VMEM((8, 48, LANES), BF16),
+            pltpu.VMEM((8, 48, LANES), BF16),
             dma((3,)),
+            dma((10,)),
             dma((4, NSEQ)),
             dma((4, NSEQ)),
             dma((2, 4, 2)),
@@ -476,24 +617,36 @@
             dma((2, 4)),
             dma((4, 8)),
             dma((4, 8)),
+            dma((8, 2)),
+            dma((8, 2)),
+            dma((2, 8)),
+            dma((2, 8)),
         ],
         compiler_params=pltpu.CompilerParams(
-            collective_id=0, has_side_effects=True, vmem_limit_bytes=48 * 1024 * 1024
+            collective_id=0, has_side_effects=True, vmem_limit_bytes=64 * 1024 * 1024
         ),
         name="monarch_block",
     )(
-        inputs[0],
-        targets[0],
+        inputs[0].T,
+        targets[0].T,
         block_mix,
         cross_mix,
         twiddle_in,
         twiddle_out,
-        norm_gain.reshape(1, D),
+        norm_gain.reshape(D // 128, 128),
         w_gate,
         w_up,
         w_down,
     )
-    return output[None], d_input[None], grad_down
+    output, d_input, grad_down = pl.pallas_call(
+        finish,
+        out_shape=results,
+        in_specs=[vmem] * 3,
+        out_specs=(vmem, vmem, vmem),
+        compiler_params=pltpu.CompilerParams(vmem_limit_bytes=64 * 1024 * 1024),
+        name="hand_over",
+    )(*made)
+    return output.T[None], d_input.T[None], grad_down
 
 
 def solution(mesh):

time: 112 us -> 91.3 us (0.82); the launches traced: 112 us -> 89.7 us
  local copies, waits for them, and re-layouts: 11.6 us -> 0 us
  Pallas kernels: 99.4 us -> 89.1 us
    unnamed x19 -> x0, local copies, waits for them, and re-layouts: 10.9 us -> none
    pallas_call x1 -> x2, Pallas kernels: 99.4 us -> 89.1 us  [the longest x1 87.5 us: body(): pl.pallas_call(kernel, out_shape=results, in_specs=[hbm] * 10, out_specs=...]
where the time goes in v2:
time: 91.3 us; the launch traced here: 89.7 us
  Pallas kernels  89.1 us (98%)
    pallas_call x1, Pallas kernels, body(): pl.pallas_call(kernel, out_shape=results, in_specs=[hbm] * 10, out_specs=...  87.5 us

profile of v2, /device:TPU:1, one launch (start us, length us, event | category | flops | bytes accessed | tf_op | source)
XLA Modules:
  0.0 89.7 jit_solution(1324478885482254983)
XLA Ops:
  0.6 87.5 %monarch_block.1 = (bf16[192,256]{1,0:T(8,128)(2,1)}, bf16[192,256]{1,0:T(8,128)(2,1)}, f32[24,384]{1,0:T(8,128)}) custom-call(bf16[192,256]{1,0:T(8,128)(2,1)} %bitcast.13, bf16[192,256]{1,0:T(8,128)(2,1)} %bitcast.14, bf16[256,256]{1,0:T(8,128)(2,1)} %bm_hbm.1, bf16[16,16]{1,0:T(8,128)(2,1)} %cm_hbm.1, f32[1,256]{1,0:T(1,128)} %ti_hbm.1, f32[16,16]{1,0:T(8,128)} %to_hbm.1, ...), custom_call_target="tpu_custom_call" | custom-call | tf_op jit(solution)/shard_map/monarch_block/pallas_call | solution.py:558
  88.1 1.6 %hand_over.1 = (bf16[192,256]{1,0:T(8,128)(2,1)}, bf16[192,256]{1,0:T(8,128)(2,1)}, f32[24,384]{1,0:T(8,128)}) custom-call(bf16[192,256]{1,0:T(8,128)(2,1)} %get-tuple-element.9.out_in, bf16[192,256]{1,0:T(8,128)(2,1)} %get-tuple-element.10.din_in, f32[24,384]{1,0:T(8,128)} %get-tuple-element.11.gd_in), custom_call_target="tpu_custom_call" | custom-call | tf_op jit(solution)/shard_map/hand_over/pallas_call | solution.py:641

commit v3 on v2

v3 whole, which is shorter than its diff:
```python
import functools

import jax
import jax.numpy as jnp
from jax import lax
from jax.experimental import pallas as pl
from jax.experimental.pallas import tpu as pltpu
from jax.sharding import PartitionSpec as P

F32 = jnp.float32
BF16 = jnp.bfloat16
MESH = pl.DeviceIdType.MESH

TOK = 256
HT = TOK // 2
CH = 192
HID = 384
NSEQ = 16
NTEN = 8
POS = 16
D = 1536
LANES = 128
ROWS = 24
EPS = 1e-05


def mm(a, b, ca=1, cb=0):
    return lax.dot_general(a, b, (((ca,), (cb,)), ((), ())), preferred_element_type=F32)


def eye(n, dtype=BF16):
    rows = lax.broadcasted_iota(jnp.int32, (n, n), 0)
    cols = lax.broadcasted_iota(jnp.int32, (n, n), 1)
    return jnp.where(rows == cols, 1.0, 0.0).astype(dtype)


def column_of(row):
    n = row.shape[1]
    return jnp.sum(eye(n, F32) * row, axis=1, keepdims=True)


def kernel(
    x_hbm, tgt_hbm, bm_hbm, cm_hbm, ti_hbm, to_hbm, gain_hbm, wg_hbm, wu_hbm, wd_hbm,
    out_hbm, din_hbm, gd_hbm,
    out_ref, din_ref, gd_ref, x_ref, tgt_ref, bm_ref, cm_ref, ti_ref, to_ref, gain_ref,
    wg, wu, wd, wguT, wdT, kron, kronT,
    a1s, a1r, a2s, a2r, a3s, a3r, a4s, a4r,
    r1, r2, v1, v2,
    p1, p2, sb1, sb2, q1, q2, t1, t2, own, gate_s, up_s, hid_s, res_s, dres_s,
    ya, yr, zb, zr, y2s, y2r, z2s, z2r,
    osem, wsem, a_ss, a_rs, ag_ss, ag_rs, sib_ss, sib_rs, v_ss, v_rs,
    rsib_ss, rsib_rs, rs_ss, rs_rs, g_ss, g_rs, g2_ss, g2_rs,
):
    dp = lax.axis_index("dp")
    sq = lax.axis_index("seq")
    tn = lax.axis_index("tensor")
    x, c = tn // 2, tn % 2
    y, zh = sq // 2, sq % 2
    z = zh * 4 + dp

    def seq_dev(s):
        return (dp, s, tn)

    def ten_dev(t):
        return (dp, sq, t)

    def y_dev(yy):
        return (dp, yy * 2 + zh, tn)

    def z_dev(zz):
        return (lax.rem(zz, 4), y * 2 + zz // 4, tn)

    pending = []

    def drain():
        while pending:
            pending.pop(0)()


    def send(src, dst, ss, rs, dev):
        cp = pltpu.make_async_remote_copy(
            src_ref=src, dst_ref=dst, send_sem=ss, recv_sem=rs, device_id=dev, device_id_type=MESH
        )
        cp.start()
        pending.append(cp.wait_send)

    def wait_recv(buf, ss, rs):
        pltpu.make_async_remote_copy(
            src_ref=buf, dst_ref=buf, send_sem=ss, recv_sem=rs,
            device_id=(dp, sq, tn), device_id_type=MESH,
        ).wait_recv()

    loads = []
    for n, (src, dst) in enumerate(
        (
            (x_hbm, x_ref), (bm_hbm, bm_ref), (ti_hbm, ti_ref), (cm_hbm, cm_ref), (to_hbm, to_ref),
            (gain_hbm, gain_ref), (wg_hbm, wg), (wu_hbm, wu), (wd_hbm, wd), (tgt_hbm, tgt_ref),
        )
    ):
        cp = pltpu.make_async_copy(src, dst, wsem.at[n])
        loads.append(cp)
    for cp in loads[0:3]:
        cp.start()

    barrier = pltpu.get_barrier_semaphore()

    def greet(dev):
        pl.semaphore_signal(barrier, inc=1, device_id=dev, device_id_type=MESH)

    def greet_seq(i, carry):
        greet(seq_dev(lax.rem(sq + i, NSEQ)))
        return carry

    def greet_ten(i, carry):
        greet(ten_dev(lax.rem(tn + i, NTEN)))
        return carry

    lax.fori_loop(1, NSEQ, greet_seq, 0)
    lax.fori_loop(1, NTEN, greet_ten, 0)
    for i in (1, 2, 3, 5, 6, 7):
        greet(z_dev(lax.rem(z + i, 8)))

    for cp in loads[3:]:
        cp.start()

    def store(n, src, dst):
        cp = pltpu.make_async_copy(src, dst, osem.at[n])
        cp.start()
        pending.append(cp.wait)

    def all_to_all_send(n, src, dst, halves=(0, 1)):
        for h in halves:

            def one(i, carry):
                peer = h * 8 + lax.rem(sq + i, 8)

                @pl.when(peer != sq)
                def _():
                    pltpu.make_async_remote_copy(
                        src_ref=src.at[peer], dst_ref=dst.at[sq],
                        send_sem=a_ss.at[n, peer], recv_sem=a_rs.at[n, sq],
                        device_id=seq_dev(peer), device_id_type=MESH,
                    ).start()

                return carry

            lax.fori_loop(0, 8, one, 0)
        if 1 in halves:
            dst[sq] = src[sq]
            pending.append(functools.partial(all_to_all_done, n, src))

    def all_to_all_wait(n, src, dst, halves=(0, 1)):
        for h in halves:

            def one(i, carry):
                peer = h * 8 + lax.rem(sq + i, 8)

                @pl.when(peer != sq)
                def _():
                    wait_recv(dst.at[peer], a_ss.at[n, peer], a_rs.at[n, peer])

                return carry

            lax.fori_loop(0, 8, one, 0)

    def all_to_all_done(n, src):
        def one(i, carry):
            peer = lax.rem(sq + i, NSEQ)
            pltpu.make_async_remote_copy(
                src_ref=src.at[peer], dst_ref=src.at[peer],
                send_sem=a_ss.at[n, peer], recv_sem=a_rs.at[n, peer],
                device_id=seq_dev(peer), device_id_type=MESH,
            ).wait_send()
            return carry

        lax.fori_loop(1, NSEQ, one, 0)

    for cp in loads[0:3]:
        cp.wait()
    tin = column_of(ti_ref[...])
    section = mm(bm_ref[...], x_ref[...], 0, 1) * tin
    a1s[...] = section.astype(BF16).reshape(NSEQ, POS, CH)

    pl.semaphore_wait(barrier, (NSEQ - 1) + (NTEN - 1) + 6)
    all_to_all_send(0, a1s, a1r)

    rows = lax.broadcasted_iota(jnp.int32, (TOK, NSEQ), 0)
    cols = lax.broadcasted_iota(jnp.int32, (TOK, NSEQ), 1)
    pick_block = jnp.where(rows // POS == cols, 1.0, 0.0)
    pick_pos = jnp.where(rows % POS == cols, 1.0, 0.0)
    for cp in loads[3:6]:
        cp.wait()
    cross = cm_ref[...]
    wide = mm(pick_block.astype(BF16), cross, 1, 1).astype(BF16)
    wide = mm(wide, pick_block.astype(BF16), 1, 1)
    wideT = mm(pick_block.astype(BF16), cross, 1, 0).astype(BF16)
    wideT = mm(wideT, pick_block.astype(BF16), 1, 1)
    big_r = lax.broadcasted_iota(jnp.int32, (TOK, TOK), 0)
    big_c = lax.broadcasted_iota(jnp.int32, (TOK, TOK), 1)
    same_pos = (big_r % POS) == (big_c % POS)
    kron[...] = jnp.where(same_pos, wide, 0.0).astype(BF16)
    kronT[...] = jnp.where(same_pos, wideT, 0.0).astype(BF16)
    tout_all = jnp.broadcast_to(to_ref[...][:, None, :], (NSEQ, POS, POS)).reshape(TOK, POS)
    tout = jnp.sum(tout_all * pick_pos, axis=1, keepdims=True)
    flat = tn * CH + lax.broadcasted_iota(jnp.int32, (CH, 128), 0)
    lane = lax.broadcasted_iota(jnp.int32, (CH, 128), 1)
    gain = jnp.zeros((CH, 128), F32)
    for k in range(D // 128):
        gain = gain + jnp.where(flat == k * 128 + lane, gain_ref[k : k + 1, :], 0.0)
    gain = jnp.sum(gain, axis=1, keepdims=True)
    for cp in loads[6:]:
        cp.wait()
    eye_h = eye(HID)
    for k in range(4):
        block = slice(k * HID, (k + 1) * HID)
        wguT[k, 0:HID, :] = mm(eye_h, wg[block, :], 1, 1).astype(BF16)
        wguT[k, HID : 2 * HID, :] = mm(eye_h, wu[block, :], 1, 1).astype(BF16)
        wdT[k] = mm(eye_h, wd[block, :], 1, 1).astype(BF16)
    eye_c = eye(CH)

    all_to_all_wait(0, a1s, a1r)

    mixed = mm(kron[...], a1r[...].reshape(TOK, CH)) * tout
    a2s[...] = mixed.astype(BF16).reshape(NSEQ, POS, CH)
    all_to_all_send(1, a2s, a2r)
    halves = [slice(0, HT), slice(HT, TOK)]

    def residual(h):
        all_to_all_wait(1, a2s, a2r, (h,))
        mixed = mm(eye_c, a2r[h * 8 : h * 8 + 8].reshape(HT, CH), 1, 1)
        res = (x_ref[:, halves[h]].astype(F32) + mixed).astype(BF16).astype(F32)
        res_s[h] = res
        r1[h, tn] = (res * gain).astype(BF16)
        gather_start(0, h, r1)
        share_row(0, h, v1, jnp.sum(res * res, axis=0, keepdims=True))

    def share_row(n, h, buf, row):
        buf[h, tn] = jnp.broadcast_to(row, (8, HT))

        def one(i, carry):
            peer = lax.rem(tn + i, NTEN)
            pltpu.make_async_remote_copy(
                src_ref=buf.at[h, tn], dst_ref=buf.at[h, tn],
                send_sem=v_ss.at[n, h, peer], recv_sem=v_rs.at[n, h, tn],
                device_id=ten_dev(peer), device_id_type=MESH,
            ).start()
            return carry

        lax.fori_loop(1, NTEN, one, 0)
        pending.append(functools.partial(rows_done, n, h, buf))

    def sum_rows(n, h, buf):
        def one(i, carry):
            peer = lax.rem(tn + i, NTEN)
            wait_recv(buf.at[h, peer], v_ss.at[n, h, peer], v_rs.at[n, h, peer])
            return carry

        lax.fori_loop(1, NTEN, one, 0)
        return jnp.sum(buf[h, :, 0:1, :], axis=0)

    def rows_done(n, h, buf):
        def one(i, carry):
            peer = lax.rem(tn + i, NTEN)
            pltpu.make_async_remote_copy(
                src_ref=buf.at[h, tn], dst_ref=buf.at[h, tn],
                send_sem=v_ss.at[n, h, peer], recv_sem=v_rs.at[n, h, peer],
                device_id=ten_dev(peer), device_id_type=MESH,
            ).wait_send()
            return carry

        lax.fori_loop(1, NTEN, one, 0)

    chips = [lax.rem(x + d, 4) for d in range(4)]
    other = 1 - c

    def gather_start(n, h, buf):
        part = buf.at[h, tn]
        for d in (2, 1, 3):
            send(part, part, ag_ss.at[n, d, h], ag_rs.at[n, d, h], ten_dev(chips[d] * 2 + c))
        send(part, part, sib_ss.at[n, 0, h], sib_rs.at[n, 0, h], ten_dev(x * 2 + other))

    def gather_forward(n, h, buf, then=None):
        for d in (1, 3, 2):
            src = lax.rem(x + 4 - d, 4) * 2 + c
            part = buf.at[h, src]
            wait_recv(part, ag_ss.at[n, d, h], ag_rs.at[n, d, h])
            send(part, part, sib_ss.at[n, d, h], sib_rs.at[n, d, h], ten_dev(x * 2 + other))
            if then is not None:
                then(src // 2, c)

    def gather_matmul(n, h, buf, weights):
        acc = None
        for d in (0, 1, 3, 2):
            chip = lax.rem(x + 4 - d, 4)
            wait_recv(buf.at[h, chip * 2 + other], sib_ss.at[n, d, h], sib_rs.at[n, d, h])
            term = mm(weights[chip], buf[h, pl.ds(chip * 2, 2)].reshape(2 * CH, HT))
            acc = term if acc is None else acc + term
        return acc

    def scatter_start(n, h, part_of, p, sb):
        for d in (2, 1, 3, 0):
            p[h, d] = part_of(chips[d] * 2 + other).astype(BF16)
            send(p.at[h, d], sb.at[h, d], rsib_ss.at[n, h, d], rsib_rs.at[n, h, d], ten_dev(x * 2 + other))
        for d in (2, 1, 3, 0):
            own[h, d] = part_of(chips[d] * 2 + c)

    def scatter_mid(n, h, sb, q, t):
        for d in (2, 1, 3):
            wait_recv(sb.at[h, d], rsib_ss.at[n, h, d], rsib_rs.at[n, h, d])
            q[h, d] = (own[h, d] + sb[h, d].astype(F32)).astype(BF16)
            send(q.at[h, d], t.at[h, d], rs_ss.at[n, h, d], rs_rs.at[n, h, d], ten_dev(chips[d] * 2 + c))

    def scatter_end(n, h, sb, t):
        wait_recv(sb.at[h, 0], rsib_ss.at[n, h, 0], rsib_rs.at[n, h, 0])
        total = own[h, 0] + sb[h, 0].astype(F32)
        for d in (1, 3, 2):
            wait_recv(t.at[h, d], rs_ss.at[n, h, d], rs_rs.at[n, h, d])
            total = total + t[h, d].astype(F32)
        return total

    def rows_of(ref, r):
        return ref[pl.ds(pl.multiple_of(r * CH, CH), CH), :]

    inv = [None, None]

    def forward(h):
        pre = gather_matmul(0, h, r1, wguT)
        inv[h] = lax.rsqrt(sum_rows(0, h, v1) / D + EPS)
        gate_pre = pre[0:HID] * inv[h]
        up_pre = pre[HID : 2 * HID] * inv[h]
        sig = jax.nn.sigmoid(gate_pre)
        hid_s[h] = (gate_pre * sig * up_pre).astype(BF16)
        gate_s[h] = gate_pre
        up_s[h] = up_pre
        scatter_start(0, h, lambda r: mm(rows_of(wd, r), hid_s[h]), p1, sb1)

    def cotangent(h):
        summed = res_s[h] + scatter_end(0, h, sb1, t1)
        r2[h, tn] = (summed - tgt_ref[:, halves[h]].astype(F32)).astype(BF16)
        gather_start(1, h, r2)
        out_ref[:, halves[h]] = summed.astype(BF16)

    def backward(h):
        d_hidden = gather_matmul(1, h, r2, wdT)
        gate_pre = gate_s[h]
        up_pre = up_s[h]
        sig = jax.nn.sigmoid(gate_pre)
        d_gate = (d_hidden * up_pre * sig * (1.0 + gate_pre * (1.0 - sig))).astype(BF16)
        d_up = (d_hidden * gate_pre * sig).astype(BF16)
        inner = d_gate.astype(F32) * gate_pre + d_up.astype(F32) * up_pre
        share_row(1, h, v2, jnp.sum(inner, axis=0, keepdims=True))
        scatter_start(1, h, lambda r: mm(rows_of(wg, r), d_gate) + mm(rows_of(wu, r), d_up), p2, sb2)

    def d_residual(h):
        d_normed = scatter_end(1, h, sb2, t2)
        corr = sum_rows(1, h, v2) / D
        d_res = r2[h, tn].astype(F32) + inv[h] * (gain * d_normed - res_s[h] * inv[h] * corr)
        dres_s[:, halves[h]] = d_res.astype(BF16)
        d_tok = mm(eye_h[0:HT, 0:HT], d_res.astype(BF16), 1, 1)
        a3s[h * 8 : h * 8 + 8] = d_tok.astype(BF16).reshape(8, POS, CH)
        all_to_all_send(2, a3s, a3r, (h,))

    sign = 1 - 2 * c

    def grad_rank(chip, yhi):
        cots = jnp.concatenate([r2[h, chip * 2 + yhi] for h in range(2)], axis=1)
        hids = jnp.concatenate([hid_s[h] for h in range(2)], axis=1)
        g = mm(cots, hids, 1, 1)
        first, second, third = (g[:, n * LANES : (n + 1) * LANES] for n in range(3))
        at = pl.multiple_of(chip * 48, 16)
        for m in range(4):
            ya[yhi * 4 + m, pl.ds(at, 48), :] = first[m * 48 : m * 48 + 48].astype(BF16)
        zat = pl.multiple_of(yhi * 96, 16)
        for half in range(2):
            pieces = [second[m * 48 + half * ROWS : m * 48 + half * ROWS + ROWS] for m in range(4)]
            zb[half * 4 + chip, pl.ds(zat, 96), :] = jnp.concatenate(pieces, axis=0).astype(BF16)

        @pl.when(chip < 2)
        def _():
            for m in range(4):
                ya[yhi * 4 + m, pl.ds(CH + at, 48), :] = third[m * 48 : m * 48 + 48].astype(BF16)

        @pl.when(chip >= 2)
        def _():
            for half in range(2):
                pieces = [third[m * 48 + half * ROWS : m * 48 + half * ROWS + ROWS] for m in range(4)]
                zb[half * 4 + chip, pl.ds(CH + zat, 96), :] = jnp.concatenate(pieces, axis=0).astype(BF16)

    def away(me, k):
        return lax.rem(me + sign * k + 8, 8)

    def sized(axis, target, work):
        if axis == 0:
            work(CH + 96)
            return

        @pl.when(lax.rem(target, 4) < 2)
        def _():
            work(CH)

        @pl.when(lax.rem(target, 4) >= 2)
        def _():
            work(2 * CH)

    AXES = ((ya, yr, y, y_dev), (zb, zr, z, z_dev))

    def grad_copy(axis, slot, to, target, rows):
        src, dst, me, dev = AXES[axis]
        return pltpu.make_async_remote_copy(
            src_ref=src.at[target, pl.ds(0, rows)], dst_ref=dst.at[slot, pl.ds(0, rows)],
            send_sem=g_ss.at[axis, slot], recv_sem=g_rs.at[axis, slot],
            device_id=dev(away(me, to)), device_id_type=MESH,
        )

    STEP1 = ((0, 2, 4), (1, 1, 3), (2, -1, -3), (3, 1, 1), (4, -1, -1))
    STEP2 = ((5, 2, 2), (6, -2, -2))

    def grad_step(axis, sends):
        me = AXES[axis][2]
        for slot, to, place in sends:
            target = away(me, place)
            sized(axis, target, lambda rows: grad_copy(axis, slot, to, target, rows).start())

            def done(slot=slot, to=to, target=target):
                sized(axis, target, lambda rows: grad_copy(axis, slot, to, target, rows).wait_send())

            pending.append(done)

    def grad_add(axis, target, slots):
        buf, got, me, dev = AXES[axis]

        def work(rows):
            total = buf[target, 0:rows, :].astype(F32)
            for slot in slots:
                part = got.at[slot, pl.ds(0, rows)]
                wait_recv(part, g_ss.at[axis, slot], g_rs.at[axis, slot])
                total = total + part[...].astype(F32)
            buf[target, 0:rows, :] = total.astype(BF16)

        sized(axis, target, work)

    def grad_first():
        for axis in range(2):
            grad_step(axis, STEP1)

    def grad_middle():
        for axis in range(2):
            me = AXES[axis][2]
            grad_add(axis, away(me, 2), (0, 1))
            grad_add(axis, away(me, -2), (2,))
            grad_step(axis, STEP2)

    def grad_second():
        total = ya[y].astype(F32)
        for slot in (3, 4, 6, 5):
            wait_recv(yr.at[slot], g_ss.at[0, slot], g_rs.at[0, slot])
            total = total + yr[slot].astype(F32)
        for zl in range(4):
            for half in range(2):
                at = zl * 48 + half * ROWS
                pieces = [total[at : at + ROWS]]
                if zl < 2:
                    pieces.append(total[CH + at : CH + at + ROWS])
                else:
                    pieces.append(jnp.zeros((ROWS, LANES), F32))
                y2s[half * 4 + zl] = jnp.concatenate(pieces, axis=0).astype(BF16)
        second_send(0, y2s, y2r, z, z_dev)

        def sum_z(rows):
            total = zb[z, 0:rows, :].astype(F32)
            for slot in (3, 4, 6, 5):
                part = zr.at[slot, pl.ds(0, rows)]
                wait_recv(part, g_ss.at[1, slot], g_rs.at[1, slot])
                total = total + part[...].astype(F32)
            for yy in range(8):
                pieces = [total[yy * ROWS : yy * ROWS + ROWS]]
                if rows > CH:
                    pieces.append(total[CH + yy * ROWS : CH + yy * ROWS + ROWS])
                else:
                    pieces.append(jnp.zeros((ROWS, LANES), F32))
                z2s[yy] = jnp.concatenate(pieces, axis=0).astype(BF16)

        sized(1, z, sum_z)
        second_send(1, z2s, z2r, y, y_dev)

    def second_send(n, src, dst, me, dev):
        def one(i, carry):
            peer = lax.rem(me + i, 8)
            pltpu.make_async_remote_copy(
                src_ref=src.at[peer], dst_ref=dst.at[me],
                send_sem=g2_ss.at[n, peer], recv_sem=g2_rs.at[n, me],
                device_id=dev(peer), device_id_type=MESH,
            ).start()
            return carry

        lax.fori_loop(1, 8, one, 0)
        pending.append(functools.partial(second_done, n, src, me, dev))

    def second_done(n, src, me, dev):
        def one(i, carry):
            peer = lax.rem(me + i, 8)
            pltpu.make_async_remote_copy(
                src_ref=src.at[peer], dst_ref=src.at[peer],
                send_sem=g2_ss.at[n, peer], recv_sem=g2_rs.at[n, peer],
                device_id=dev(peer), device_id_type=MESH,
            ).wait_send()
            return carry

        lax.fori_loop(1, 8, one, 0)

    def second_sum(n, src, dst, me):
        def add(i, acc):
            peer = lax.rem(me + i, 8)
            wait_recv(dst.at[peer], g2_ss.at[n, peer], g2_rs.at[n, peer])
            return acc + dst[peer].astype(F32)

        return lax.fori_loop(1, 8, add, src[me].astype(F32))

    residual(0)
    residual(1)
    gather_forward(0, 0, r1)
    forward(0)
    gather_forward(0, 1, r1)
    scatter_mid(0, 0, sb1, q1, t1)
    forward(1)
    scatter_mid(0, 1, sb1, q1, t1)
    cotangent(0)
    cotangent(1)
    store(0, out_ref, out_hbm)
    grad_rank(x, c)
    gather_forward(1, 0, r2)
    backward(0)
    gather_forward(1, 1, r2)
    scatter_mid(1, 0, sb2, q2, t2)
    backward(1)
    for d in (1, 3, 2):
        grad_rank(chips[d], c)
    scatter_mid(1, 1, sb2, q2, t2)
    for d in (0, 1, 3, 2):
        grad_rank(chips[d], other)
    grad_first()
    d_residual(0)
    d_residual(1)
    grad_middle()

    all_to_all_wait(2, a3s, a3r)
    weighted = (a3r[...].reshape(TOK, CH).astype(F32) * tout).astype(BF16)
    a4s[...] = mm(kronT[...], weighted).astype(BF16).reshape(NSEQ, POS, CH)
    all_to_all_send(3, a4s, a4r)
    grad_second()
    drain()

    rows_y = second_sum(0, y2s, y2r, z)
    rows_z = second_sum(1, z2s, z2r, y)
    gd_ref[:, 0:LANES] = rows_y[0:ROWS]
    gd_ref[:, LANES : 2 * LANES] = rows_z[0:ROWS]
    gd_ref[:, 2 * LANES : HID] = rows_y[ROWS:48] + rows_z[ROWS:48]
    store(2, gd_ref, gd_hbm)

    all_to_all_wait(3, a4s, a4r)
    scaled = (a4r[...].reshape(TOK, CH).astype(F32) * tin).astype(BF16)
    d_mix = mm(scaled, bm_ref[...], 0, 1)
    din_ref[...] = (dres_s[...].astype(F32) + d_mix).astype(BF16)

    store(1, din_ref, din_hbm)

    drain()


def finish(out_in, din_in, gd_in, out_ref, din_ref, gd_ref):
    out_ref[...] = out_in[...]
    din_ref[...] = din_in[...]
    gd_ref[...] = gd_in[...]


def body(
    inputs, targets, block_mix, cross_mix, twiddle_in, twiddle_out, norm_gain, w_gate, w_up, w_down
):
    hbm = pl.BlockSpec(memory_space=pltpu.HBM)
    vmem = pl.BlockSpec(memory_space=pltpu.VMEM)
    dma = pltpu.SemaphoreType.DMA
    chunks = pltpu.VMEM((NSEQ, POS, CH), BF16)
    blocks4 = pltpu.VMEM((2, 4, CH, HT), BF16)
    results = (
        jax.ShapeDtypeStruct((CH, TOK), BF16),
        jax.ShapeDtypeStruct((CH, TOK), BF16),
        jax.ShapeDtypeStruct((ROWS, HID), F32),
    )
    made = pl.pallas_call(
        kernel,
        out_shape=results,
        in_specs=[hbm] * 10,
        out_specs=(hbm, hbm, hbm),
        scratch_shapes=[
            pltpu.VMEM((CH, TOK), BF16),
            pltpu.VMEM((CH, TOK), BF16),
            pltpu.VMEM((ROWS, HID), F32),
            pltpu.VMEM((CH, TOK), BF16),
            pltpu.VMEM((CH, TOK), BF16),
            pltpu.VMEM((TOK, TOK), BF16),
            pltpu.VMEM((NSEQ, NSEQ), BF16),
            pltpu.VMEM((1, TOK), F32),
            pltpu.VMEM((NSEQ, POS), F32),
            pltpu.VMEM((D // 128, 128), F32),
            pltpu.VMEM((D, HID), BF16),
            pltpu.VMEM((D, HID), BF16),
            pltpu.VMEM((D, HID), BF16),
            pltpu.VMEM((4, 2 * HID, HID), BF16),
            pltpu.VMEM((4, HID, HID), BF16),
            pltpu.VMEM((TOK, TOK), BF16),
            pltpu.VMEM((TOK, TOK), BF16),
        ]
        + [chunks] * 8
        + [
            pltpu.VMEM((2, NTEN, CH, HT), BF16),
            pltpu.VMEM((2, NTEN, CH, HT), BF16),
            pltpu.VMEM((2, NTEN, 8, HT), F32),
            pltpu.VMEM((2, NTEN, 8, HT), F32),
        ]
        + [blocks4] * 8
        + [
            pltpu.VMEM((2, 4, CH, HT), F32),
            pltpu.VMEM((2, HID, HT), F32),
            pltpu.VMEM((2, HID, HT), F32),
            pltpu.VMEM((2, HID, HT), BF16),
            pltpu.VMEM((2, CH, HT), F32),
            pltpu.VMEM((CH, TOK), BF16),
            pltpu.VMEM((8, CH + 96, LANES), BF16),
            pltpu.VMEM((7, CH + 96, LANES), BF16),
            pltpu.VMEM((8, 2 * CH, LANES), BF16),
            pltpu.VMEM((7, 2 * CH, LANES), BF16),
            pltpu.VMEM((8, 48, LANES), BF16),
            pltpu.VMEM((8, 48, LANES), BF16),
            pltpu.VMEM((8, 48, LANES), BF16),
            pltpu.VMEM((8, 48, LANES), BF16),
            dma((3,)),
            dma((10,)),
            dma((4, NSEQ)),
            dma((4, NSEQ)),
            dma((2, 4, 2)),
            dma((2, 4, 2)),
            dma((2, 4, 2)),
            dma((2, 4, 2)),
            dma((2, 2, NTEN)),
            dma((2, 2, NTEN)),
            dma((2, 2, 4)),
            dma((2, 2, 4)),
            dma((2, 2, 4)),
            dma((2, 2, 4)),
            dma((2, 7)),
            dma((2, 7)),
            dma((2, 8)),
            dma((2, 8)),
        ],
        compiler_params=pltpu.CompilerParams(
            collective_id=0, has_side_effects=True, vmem_limit_bytes=64 * 1024 * 1024
        ),
        name="monarch_block",
    )(
        inputs[0].T,
        targets[0].T,
        block_mix,
        cross_mix,
        twiddle_in,
        twiddle_out,
        norm_gain.reshape(D // 128, 128),
        w_gate,
        w_up,
        w_down,
    )
    output, d_input, grad_down = pl.pallas_call(
        finish,
        out_shape=results,
        in_specs=[vmem] * 3,
        out_specs=(vmem, vmem, vmem),
        compiler_params=pltpu.CompilerParams(vmem_limit_bytes=64 * 1024 * 1024),
        name="hand_over",
    )(*made)
    return output.T[None], d_input.T[None], grad_down


def solution(mesh):
    return jax.shard_map(
        body,
        mesh=mesh,
        in_specs=(
            P("dp", "seq", "tensor"),
            P("dp", "seq", "tensor"),
            P(),
            P(),
            P("seq", None),
            P(None, "seq"),
            P(),
            P(None, "tensor"),
            P(None, "tensor"),
            P(None, "tensor"),
        ),
        out_specs=(P("dp", "seq", "tensor"), P("dp", "seq", "tensor"), P(("dp", "seq"), "tensor")),
        check_vma=False,
    )
```

time: 91.3 us -> 86.2 us (0.944)
  Pallas kernels: 89.1 us -> 84 us
    pallas_call x1, Pallas kernels: 87.5 us -> 82.3 us  [body(): pl.pallas_call(kernel, out_shape=results, in_specs=[hbm] * 10, out_specs=...]
where the time goes in v3:
time: 86.2 us; the launch traced here: 84.6 us
  Pallas kernels  84 us (97%)
    pallas_call x1, Pallas kernels, body(): pl.pallas_call(kernel, out_shape=results, in_specs=[hbm] * 10, out_specs=...  82.3 us

profile of v3, /device:TPU:1, one launch (start us, length us, event | category | flops | bytes accessed | tf_op | source)
XLA Modules:
  0.0 84.6 jit_solution(7672883398195121937)
XLA Ops:
  0.6 82.3 %monarch_block.1 = (bf16[192,256]{1,0:T(8,128)(2,1)}, bf16[192,256]{1,0:T(8,128)(2,1)}, f32[24,384]{1,0:T(8,128)}) custom-call(bf16[192,256]{1,0:T(8,128)(2,1)} %bitcast.13, bf16[192,256]{1,0:T(8,128)(2,1)} %bitcast.14, bf16[256,256]{1,0:T(8,128)(2,1)} %bm_hbm.1, bf16[16,16]{1,0:T(8,128)(2,1)} %cm_hbm.1, f32[1,256]{1,0:T(1,128)} %ti_hbm.1, f32[16,16]{1,0:T(8,128)} %to_hbm.1, ...), custom_call_target="tpu_custom_call" | custom-call | tf_op jit(solution)/shard_map/monarch_block/pallas_call | solution.py:589
  83.0 1.6 %hand_over.1 = (bf16[192,256]{1,0:T(8,128)(2,1)}, bf16[192,256]{1,0:T(8,128)(2,1)}, f32[24,384]{1,0:T(8,128)}) custom-call(bf16[192,256]{1,0:T(8,128)(2,1)} %get-tuple-element.9.out_in, bf16[192,256]{1,0:T(8,128)(2,1)} %get-tuple-element.10.din_in, f32[24,384]{1,0:T(8,128)} %get-tuple-element.11.gd_in), custom_call_target="tpu_custom_call" | custom-call | tf_op jit(solution)/shard_map/hand_over/pallas_call | solution.py:671

commit v4 on v3

--- a/solution.py
+++ b/solution.py
@@ -18,6 +18,8 @@
 NSEQ = 16
 NTEN = 8
 POS = 16
+LINE = 32
+FAR_FIRST = (4, 3, 5, 2, 6, 1, 7)
 D = 1536
 LANES = 128
 ROWS = 24
@@ -48,7 +50,7 @@
     r1, r2, v1, v2,
     p1, p2, sb1, sb2, q1, q2, t1, t2, own, gate_s, up_s, hid_s, res_s, dres_s,
     ya, yr, zb, zr, y2s, y2r, z2s, z2r,
-    osem, wsem, a_ss, a_rs, ag_ss, ag_rs, sib_ss, sib_rs, v_ss, v_rs,
+    to_pair, cross_sem, tw_sem, osem, wsem, a_ss, a_rs, ag_ss, ag_rs, sib_ss, sib_rs, v_ss, v_rs,
     rsib_ss, rsib_rs, rs_ss, rs_rs, g_ss, g_rs, g2_ss, g2_rs,
 ):
     dp = lax.axis_index("dp")
@@ -107,19 +109,11 @@
     def greet(dev):
         pl.semaphore_signal(barrier, inc=1, device_id=dev, device_id_type=MESH)
 
-    def greet_seq(i, carry):
-        greet(seq_dev(lax.rem(sq + i, NSEQ)))
-        return carry
-
-    def greet_ten(i, carry):
+    for i in FAR_FIRST:
+        greet(y_dev(lax.rem(y + i, 8)))
+        greet(z_dev(lax.rem(z + i, 8)))
+    for i in (4, 5, 3, 6, 2, 7, 1):
         greet(ten_dev(lax.rem(tn + i, NTEN)))
-        return carry
-
-    lax.fori_loop(1, NSEQ, greet_seq, 0)
-    lax.fori_loop(1, NTEN, greet_ten, 0)
-    for i in (1, 2, 3, 5, 6, 7):
-        greet(z_dev(lax.rem(z + i, 8)))
-
     for cp in loads[3:]:
         cp.start()
 
@@ -128,26 +122,34 @@
         cp.start()
         pending.append(cp.wait)
 
-    def all_to_all_send(n, src, dst, halves=(0, 1)):
-        for h in halves:
-
-            def one(i, carry):
-                peer = h * 8 + lax.rem(sq + i, 8)
-
-                @pl.when(peer != sq)
-                def _():
-                    pltpu.make_async_remote_copy(
-                        src_ref=src.at[peer], dst_ref=dst.at[sq],
-                        send_sem=a_ss.at[n, peer], recv_sem=a_rs.at[n, sq],
-                        device_id=seq_dev(peer), device_id_type=MESH,
-                    ).start()
-
-                return carry
-
-            lax.fori_loop(0, 8, one, 0)
-        if 1 in halves:
+    def a2a_copy(n, src, dst, peer):
+        return pltpu.make_async_remote_copy(
+            src_ref=src.at[peer], dst_ref=dst.at[sq],
+            send_sem=a_ss.at[n, peer], recv_sem=a_rs.at[n, sq],
+            device_id=seq_dev(peer), device_id_type=MESH,
+        )
+
+    def all_to_all_send(n, src, dst):
+        for i in FAR_FIRST + (0,):
+            yy = lax.rem(y + i, 8)
+            a2a_copy(n, src, dst, yy * 2 + 1 - zh).start()
+            if i:
+                a2a_copy(n, src, dst, yy * 2 + zh).start()
+        dst[sq] = src[sq]
+        pending.append(functools.partial(all_to_all_done, n, src, dst))
+
+    def all_to_all_send_half(n, src, dst, h):
+        for i in (2, 1, 3, 0):
+            yy = h * 4 + lax.rem(y + i, 4)
+            a2a_copy(n, src, dst, yy * 2 + 1 - zh).start()
+
+            @pl.when(yy != y)
+            def _():
+                a2a_copy(n, src, dst, yy * 2 + zh).start()
+
+        if h:
             dst[sq] = src[sq]
-            pending.append(functools.partial(all_to_all_done, n, src))
+            pending.append(functools.partial(all_to_all_done, n, src, dst))
 
     def all_to_all_wait(n, src, dst, halves=(0, 1)):
         for h in halves:
@@ -163,43 +165,64 @@
 
             lax.fori_loop(0, 8, one, 0)
 
-    def all_to_all_done(n, src):
+    def all_to_all_done(n, src, dst):
         def one(i, carry):
-            peer = lax.rem(sq + i, NSEQ)
-            pltpu.make_async_remote_copy(
-                src_ref=src.at[peer], dst_ref=src.at[peer],
-                send_sem=a_ss.at[n, peer], recv_sem=a_rs.at[n, peer],
-                device_id=seq_dev(peer), device_id_type=MESH,
-            ).wait_send()
+            a2a_copy(n, src, dst, lax.rem(sq + i, NSEQ)).wait_send()
             return carry
 
         lax.fori_loop(1, NSEQ, one, 0)
+
+    def line_copy(peer):
+        return pltpu.make_async_remote_copy(
+            src_ref=a1s.at[peer], dst_ref=a1r.at[y],
+            send_sem=a_ss.at[0, peer], recv_sem=a_rs.at[0, y],
+            device_id=y_dev(peer), device_id_type=MESH,
+        )
+
+    def line_done():
+        for i in FAR_FIRST:
+            line_copy(lax.rem(y + i, 8)).wait_send()
 
     for cp in loads[0:3]:
         cp.wait()
     tin = column_of(ti_ref[...])
     section = mm(bm_ref[...], x_ref[...], 0, 1) * tin
-    a1s[...] = section.astype(BF16).reshape(NSEQ, POS, CH)
-
-    pl.semaphore_wait(barrier, (NSEQ - 1) + (NTEN - 1) + 6)
-    all_to_all_send(0, a1s, a1r)
+    a1s[...] = section.astype(BF16).reshape(8, LINE, CH)
+
+    pl.semaphore_wait(barrier, 7 + 7 + (NTEN - 1))
+    partner = (dp, y * 2 + 1 - zh, tn)
+    for i in FAR_FIRST:
+        line_copy(lax.rem(y + i, 8)).start()
+    pending.append(line_done)
+    a1r[y] = a1s[y]
+    pl.semaphore_signal(cross_sem, inc=1, device_id=partner, device_id_type=MESH)
+    loads[4].wait()
+    to_pair[zh] = to_ref[...]
+    send(to_pair.at[zh], to_pair.at[zh], tw_sem.at[0], tw_sem.at[1], partner)
 
     rows = lax.broadcasted_iota(jnp.int32, (TOK, NSEQ), 0)
     cols = lax.broadcasted_iota(jnp.int32, (TOK, NSEQ), 1)
-    pick_block = jnp.where(rows // POS == cols, 1.0, 0.0)
+    loads[3].wait()
+    loads[5].wait()
+    cross = cm_ref[...]
+
+    def iota(shape, dim):
+        return lax.broadcasted_iota(jnp.int32, shape, dim)
+
+    def flags(hit):
+        return jnp.where(hit, 1.0, 0.0).astype(BF16)
+
+    rows_here = flags(iota((8, NSEQ), 1) == 2 * iota((8, NSEQ), 0) + zh)
+    cross_here = mm(rows_here, cross).astype(BF16)
+    wide = mm(flags(iota((NSEQ * LINE, NSEQ), 0) // LINE == iota((NSEQ * LINE, NSEQ), 1)), cross_here, 1, 1)
+    wide = mm(wide.astype(BF16), flags(iota((8, TOK), 1) // LINE == iota((8, TOK), 0)))
+    same_pos = iota((NSEQ * LINE, TOK), 0) % LINE == iota((NSEQ * LINE, TOK), 1) % LINE
+    kron[...] = jnp.where(same_pos, wide, 0.0).astype(BF16)
+    pick_block = flags(rows // POS == cols)
     pick_pos = jnp.where(rows % POS == cols, 1.0, 0.0)
-    for cp in loads[3:6]:
-        cp.wait()
-    cross = cm_ref[...]
-    wide = mm(pick_block.astype(BF16), cross, 1, 1).astype(BF16)
-    wide = mm(wide, pick_block.astype(BF16), 1, 1)
-    wideT = mm(pick_block.astype(BF16), cross, 1, 0).astype(BF16)
-    wideT = mm(wideT, pick_block.astype(BF16), 1, 1)
-    big_r = lax.broadcasted_iota(jnp.int32, (TOK, TOK), 0)
-    big_c = lax.broadcasted_iota(jnp.int32, (TOK, TOK), 1)
-    same_pos = (big_r % POS) == (big_c % POS)
-    kron[...] = jnp.where(same_pos, wide, 0.0).astype(BF16)
-    kronT[...] = jnp.where(same_pos, wideT, 0.0).astype(BF16)
+    wide = mm(mm(pick_block, cross).astype(BF16), pick_block, 1, 1)
+    same_pos = iota((TOK, TOK), 0) % POS == iota((TOK, TOK), 1) % POS
+    kronT[...] = jnp.where(same_pos, wide, 0.0).astype(BF16)
     tout_all = jnp.broadcast_to(to_ref[...][:, None, :], (NSEQ, POS, POS)).reshape(TOK, POS)
     tout = jnp.sum(tout_all * pick_pos, axis=1, keepdims=True)
     flat = tn * CH + lax.broadcasted_iota(jnp.int32, (CH, 128), 0)
@@ -218,16 +241,28 @@
         wdT[k] = mm(eye_h, wd[block, :], 1, 1).astype(BF16)
     eye_c = eye(CH)
 
-    all_to_all_wait(0, a1s, a1r)
-
-    mixed = mm(kron[...], a1r[...].reshape(TOK, CH)) * tout
-    a2s[...] = mixed.astype(BF16).reshape(NSEQ, POS, CH)
+    wait_recv(to_pair.at[1 - zh], tw_sem.at[0], tw_sem.at[1])
+    tline = jnp.zeros((NSEQ * LINE, 1), F32)
+    for half in range(2):
+        spread = jnp.broadcast_to(to_pair[half][:, None, :], (NSEQ, LINE, POS)).reshape(NSEQ * LINE, POS)
+        here = iota((NSEQ * LINE, POS), 0) % LINE == half * POS + iota((NSEQ * LINE, POS), 1)
+        tline = tline + jnp.sum(jnp.where(here, spread, 0.0), axis=1, keepdims=True)
+    pl.semaphore_wait(cross_sem, 1)
+    for i in FAR_FIRST:
+        peer = lax.rem(y + i, 8)
+        wait_recv(a1r.at[peer], a_ss.at[0, peer], a_rs.at[0, peer])
+
+    mixed = mm(kron[...], a1r[...].reshape(TOK, CH)) * tline
+    a2s[...] = mixed.astype(BF16).reshape(NSEQ, LINE, CH)
     all_to_all_send(1, a2s, a2r)
+
     halves = [slice(0, HT), slice(HT, TOK)]
 
     def residual(h):
         all_to_all_wait(1, a2s, a2r, (h,))
-        mixed = mm(eye_c, a2r[h * 8 : h * 8 + 8].reshape(HT, CH), 1, 1)
+        terms = a2r[h * 8 : h * 8 + 8].astype(F32).reshape(4, 2, LINE, CH)
+        mixed = (terms[:, 0] + terms[:, 1]).astype(BF16).reshape(HT, CH)
+        mixed = mm(eye_c, mixed, 1, 1)
         res = (x_ref[:, halves[h]].astype(F32) + mixed).astype(BF16).astype(F32)
         res_s[h] = res
         r1[h, tn] = (res * gain).astype(BF16)
@@ -358,7 +393,7 @@
         dres_s[:, halves[h]] = d_res.astype(BF16)
         d_tok = mm(eye_h[0:HT, 0:HT], d_res.astype(BF16), 1, 1)
         a3s[h * 8 : h * 8 + 8] = d_tok.astype(BF16).reshape(8, POS, CH)
-        all_to_all_send(2, a3s, a3r, (h,))
+        all_to_all_send_half(2, a3s, a3r, h)
 
     sign = 1 - 2 * c
 
@@ -607,10 +642,12 @@
             pltpu.VMEM((D, HID), BF16),
             pltpu.VMEM((4, 2 * HID, HID), BF16),
             pltpu.VMEM((4, HID, HID), BF16),
-            pltpu.VMEM((TOK, TOK), BF16),
+            pltpu.VMEM((NSEQ * LINE, TOK), BF16),
             pltpu.VMEM((TOK, TOK), BF16),
         ]
-        + [chunks] * 8
+        + [pltpu.VMEM((8, LINE, CH), BF16)] * 2
+        + [pltpu.VMEM((NSEQ, LINE, CH), BF16)] * 2
+        + [chunks] * 4
         + [
             pltpu.VMEM((2, NTEN, CH, HT), BF16),
             pltpu.VMEM((2, NTEN, CH, HT), BF16),
@@ -633,6 +670,9 @@
             pltpu.VMEM((8, 48, LANES), BF16),
             pltpu.VMEM((8, 48, LANES), BF16),
             pltpu.VMEM((8, 48, LANES), BF16),
+            pltpu.VMEM((2, NSEQ, POS), F32),
+            pltpu.SemaphoreType.REGULAR,
+            dma((2,)),
             dma((3,)),
             dma((10,)),
             dma((4, NSEQ)),

time: 86.2 us -> 84.8 us (0.984)
  the two profiles are of different devices: /device:TPU:1 before, /device:TPU:128 now
where the time goes in v4:
time: 84.8 us; the launch traced here: 84.7 us
  Pallas kernels  84.1 us (99%)
    pallas_call x1, Pallas kernels, body(): pl.pallas_call(kernel, out_shape=results, in_specs=[hbm] * 10, out_specs=...  82.4 us

profile of v4, /device:TPU:128, one launch (start us, length us, event | category | flops | bytes accessed | tf_op | source)
XLA Modules:
  0.0 84.7 jit_solution(3422635561525154506)
XLA Ops:
  0.6 82.4 %monarch_block.1 = (bf16[192,256]{1,0:T(8,128)(2,1)}, bf16[192,256]{1,0:T(8,128)(2,1)}, f32[24,384]{1,0:T(8,128)}) custom-call(bf16[192,256]{1,0:T(8,128)(2,1)} %bitcast.13, bf16[192,256]{1,0:T(8,128)(2,1)} %bitcast.14, bf16[256,256]{1,0:T(8,128)(2,1)} %bm_hbm.1, bf16[16,16]{1,0:T(8,128)(2,1)} %cm_hbm.1, f32[1,256]{1,0:T(1,128)} %ti_hbm.1, f32[16,16]{1,0:T(8,128)} %to_hbm.1, ...), custom_call_target="tpu_custom_call" | custom-call | tf_op jit(solution)/shard_map/monarch_block/pallas_call | solution.py:624
  83.1 1.6 %hand_over.1 = (bf16[192,256]{1,0:T(8,128)(2,1)}, bf16[192,256]{1,0:T(8,128)(2,1)}, f32[24,384]{1,0:T(8,128)}) custom-call(bf16[192,256]{1,0:T(8,128)(2,1)} %get-tuple-element.9.out_in, bf16[192,256]{1,0:T(8,128)(2,1)} %get-tuple-element.10.din_in, f32[24,384]{1,0:T(8,128)} %get-tuple-element.11.gd_in), custom_call_target="tpu_custom_call" | custom-call | tf_op jit(solution)/shard_map/hand_over/pallas_call | solution.py:711

commit v5 on v4

--- a/solution.py
+++ b/solution.py
@@ -18,6 +18,7 @@
 NSEQ = 16
 NTEN = 8
 POS = 16
+PACKED = 48
 LINE = 32
 FAR_FIRST = (4, 3, 5, 2, 6, 1, 7)
 D = 1536
@@ -151,19 +152,24 @@
             dst[sq] = src[sq]
             pending.append(functools.partial(all_to_all_done, n, src, dst))
 
-    def all_to_all_wait(n, src, dst, halves=(0, 1)):
-        for h in halves:
-
-            def one(i, carry):
-                peer = h * 8 + lax.rem(sq + i, 8)
-
-                @pl.when(peer != sq)
-                def _():
+    def all_to_all_wait(n, src, dst):
+        for i in (0, 7, 1, 6, 2, 5, 3, 4):
+            for other_line in range(2):
+                if i or other_line:
+                    peer = lax.rem(y + i, 8) * 2 + (1 - zh if other_line else zh)
                     wait_recv(dst.at[peer], a_ss.at[n, peer], a_rs.at[n, peer])
 
-                return carry
-
-            lax.fori_loop(0, 8, one, 0)
+    def all_to_all_wait_half(n, src, dst, h):
+        for i in (0, 3, 1, 2):
+            yy = h * 4 + lax.rem(y + i, 4)
+
+            @pl.when(yy != y)
+            def _():
+                peer = yy * 2 + zh
+                wait_recv(dst.at[peer], a_ss.at[n, peer], a_rs.at[n, peer])
+
+            peer = yy * 2 + 1 - zh
+            wait_recv(dst.at[peer], a_ss.at[n, peer], a_rs.at[n, peer])
 
     def all_to_all_done(n, src, dst):
         def one(i, carry):
@@ -189,21 +195,10 @@
     section = mm(bm_ref[...], x_ref[...], 0, 1) * tin
     a1s[...] = section.astype(BF16).reshape(8, LINE, CH)
 
-    pl.semaphore_wait(barrier, 7 + 7 + (NTEN - 1))
-    partner = (dp, y * 2 + 1 - zh, tn)
-    for i in FAR_FIRST:
-        line_copy(lax.rem(y + i, 8)).start()
-    pending.append(line_done)
-    a1r[y] = a1s[y]
-    pl.semaphore_signal(cross_sem, inc=1, device_id=partner, device_id_type=MESH)
-    loads[4].wait()
-    to_pair[zh] = to_ref[...]
-    send(to_pair.at[zh], to_pair.at[zh], tw_sem.at[0], tw_sem.at[1], partner)
-
     rows = lax.broadcasted_iota(jnp.int32, (TOK, NSEQ), 0)
     cols = lax.broadcasted_iota(jnp.int32, (TOK, NSEQ), 1)
-    loads[3].wait()
-    loads[5].wait()
+    for cp in loads[3:6]:
+        cp.wait()
     cross = cm_ref[...]
 
     def iota(shape, dim):
@@ -231,14 +226,25 @@
     for k in range(D // 128):
         gain = gain + jnp.where(flat == k * 128 + lane, gain_ref[k : k + 1, :], 0.0)
     gain = jnp.sum(gain, axis=1, keepdims=True)
+
+    pl.semaphore_wait(barrier, 7 + 7 + (NTEN - 1))
+    partner = (dp, y * 2 + 1 - zh, tn)
+    for i in FAR_FIRST:
+        line_copy(lax.rem(y + i, 8)).start()
+    pending.append(line_done)
+    a1r[y] = a1s[y]
+    pl.semaphore_signal(cross_sem, inc=1, device_id=partner, device_id_type=MESH)
+    to_pair[zh] = to_ref[...]
+    send(to_pair.at[zh], to_pair.at[zh], tw_sem.at[0], tw_sem.at[1], partner)
+
     for cp in loads[6:]:
         cp.wait()
     eye_h = eye(HID)
-    for k in range(4):
-        block = slice(k * HID, (k + 1) * HID)
-        wguT[k, 0:HID, :] = mm(eye_h, wg[block, :], 1, 1).astype(BF16)
-        wguT[k, HID : 2 * HID, :] = mm(eye_h, wu[block, :], 1, 1).astype(BF16)
-        wdT[k] = mm(eye_h, wd[block, :], 1, 1).astype(BF16)
+    for r in range(NTEN):
+        block = slice(r * CH, (r + 1) * CH)
+        wguT[r, 0:HID, :] = mm(eye_h, wg[block, :], 1, 1).astype(BF16)
+        wguT[r, HID : 2 * HID, :] = mm(eye_h, wu[block, :], 1, 1).astype(BF16)
+        wdT[r] = mm(eye_h, wd[block, :], 1, 1).astype(BF16)
     eye_c = eye(CH)
 
     wait_recv(to_pair.at[1 - zh], tw_sem.at[0], tw_sem.at[1])
@@ -253,15 +259,22 @@
         wait_recv(a1r.at[peer], a_ss.at[0, peer], a_rs.at[0, peer])
 
     mixed = mm(kron[...], a1r[...].reshape(TOK, CH)) * tline
-    a2s[...] = mixed.astype(BF16).reshape(NSEQ, LINE, CH)
+    mixed = mixed.reshape(NSEQ, LINE, CH)
+    a2s[:, 0:LINE, :] = mixed[:, :, 0:LANES].astype(BF16)
+    rest = mixed[:, :, LANES:CH]
+    rest = jnp.concatenate([rest[:, 0:POS], rest[:, POS:LINE]], axis=2)
+    a2s[:, LINE:PACKED, :] = rest.astype(BF16)
     all_to_all_send(1, a2s, a2r)
 
     halves = [slice(0, HT), slice(HT, TOK)]
 
     def residual(h):
-        all_to_all_wait(1, a2s, a2r, (h,))
-        terms = a2r[h * 8 : h * 8 + 8].astype(F32).reshape(4, 2, LINE, CH)
-        mixed = (terms[:, 0] + terms[:, 1]).astype(BF16).reshape(HT, CH)
+        all_to_all_wait_half(1, a2s, a2r, h)
+        terms = a2r[h * 8 : h * 8 + 8].astype(F32).reshape(4, 2, PACKED, LANES)
+        terms = terms[:, 0] + terms[:, 1]
+        rest = terms[:, LINE:PACKED]
+        rest = jnp.concatenate([rest[:, :, 0 : CH - LANES], rest[:, :, CH - LANES : LANES]], axis=1)
+        mixed = jnp.concatenate([terms[:, 0:LINE], rest], axis=2).astype(BF16).reshape(HT, CH)
         mixed = mm(eye_c, mixed, 1, 1)
         res = (x_ref[:, halves[h]].astype(F32) + mixed).astype(BF16).astype(F32)
         res_s[h] = res
@@ -272,25 +285,19 @@
     def share_row(n, h, buf, row):
         buf[h, tn] = jnp.broadcast_to(row, (8, HT))
 
-        def one(i, carry):
+        for i in (4, 5, 3, 6, 2, 7, 1):
             peer = lax.rem(tn + i, NTEN)
             pltpu.make_async_remote_copy(
                 src_ref=buf.at[h, tn], dst_ref=buf.at[h, tn],
                 send_sem=v_ss.at[n, h, peer], recv_sem=v_rs.at[n, h, tn],
                 device_id=ten_dev(peer), device_id_type=MESH,
             ).start()
-            return carry
-
-        lax.fori_loop(1, NTEN, one, 0)
         pending.append(functools.partial(rows_done, n, h, buf))
 
     def sum_rows(n, h, buf):
-        def one(i, carry):
+        for i in range(1, NTEN):
             peer = lax.rem(tn + i, NTEN)
             wait_recv(buf.at[h, peer], v_ss.at[n, h, peer], v_rs.at[n, h, peer])
-            return carry
-
-        lax.fori_loop(1, NTEN, one, 0)
         return jnp.sum(buf[h, :, 0:1, :], axis=0)
 
     def rows_done(n, h, buf):
@@ -326,10 +333,13 @@
     def gather_matmul(n, h, buf, weights):
         acc = None
         for d in (0, 1, 3, 2):
-            chip = lax.rem(x + 4 - d, 4)
-            wait_recv(buf.at[h, chip * 2 + other], sib_ss.at[n, d, h], sib_rs.at[n, d, h])
-            term = mm(weights[chip], buf[h, pl.ds(chip * 2, 2)].reshape(2 * CH, HT))
+            rank = lax.rem(x + 4 - d, 4) * 2 + c
+            term = mm(weights[rank], buf[h, rank])
             acc = term if acc is None else acc + term
+        for d in (0, 1, 3, 2):
+            rank = lax.rem(x + 4 - d, 4) * 2 + other
+            wait_recv(buf.at[h, rank], sib_ss.at[n, d, h], sib_rs.at[n, d, h])
+            acc = acc + mm(weights[rank], buf[h, rank])
         return acc
 
     def scatter_start(n, h, part_of, p, sb):
@@ -447,8 +457,9 @@
             device_id=dev(away(me, to)), device_id_type=MESH,
         )
 
-    STEP1 = ((0, 2, 4), (1, 1, 3), (2, -1, -3), (3, 1, 1), (4, -1, -1))
-    STEP2 = ((5, 2, 2), (6, -2, -2))
+    STEP1 = ((0, 2, 4), (1, 1, 3), (2, -1, -3))
+    STEP2 = ((3, 1, 1), (4, -1, -1))
+    STEP3 = ((5, 2, 2), (6, -2, -2))
 
     def grad_step(axis, sends):
         me = AXES[axis][2]
@@ -480,10 +491,12 @@
 
     def grad_middle():
         for axis in range(2):
+            grad_step(axis, STEP2)
+        for axis in range(2):
             me = AXES[axis][2]
             grad_add(axis, away(me, 2), (0, 1))
             grad_add(axis, away(me, -2), (2,))
-            grad_step(axis, STEP2)
+            grad_step(axis, STEP3)
 
     def grad_second():
         total = ya[y].astype(F32)
@@ -519,16 +532,13 @@
         second_send(1, z2s, z2r, y, y_dev)
 
     def second_send(n, src, dst, me, dev):
-        def one(i, carry):
+        for i in FAR_FIRST:
             peer = lax.rem(me + i, 8)
             pltpu.make_async_remote_copy(
                 src_ref=src.at[peer], dst_ref=dst.at[me],
                 send_sem=g2_ss.at[n, peer], recv_sem=g2_rs.at[n, me],
                 device_id=dev(peer), device_id_type=MESH,
             ).start()
-            return carry
-
-        lax.fori_loop(1, 8, one, 0)
         pending.append(functools.partial(second_done, n, src, me, dev))
 
     def second_done(n, src, me, dev):
@@ -544,12 +554,12 @@
         lax.fori_loop(1, 8, one, 0)
 
     def second_sum(n, src, dst, me):
-        def add(i, acc):
+        total = src[me].astype(F32)
+        for i in (7, 1, 6, 2, 5, 3, 4):
             peer = lax.rem(me + i, 8)
             wait_recv(dst.at[peer], g2_ss.at[n, peer], g2_rs.at[n, peer])
-            return acc + dst[peer].astype(F32)
-
-        return lax.fori_loop(1, 8, add, src[me].astype(F32))
+            total = total + dst[peer].astype(F32)
+        return total
 
     residual(0)
     residual(1)
@@ -573,10 +583,14 @@
     scatter_mid(1, 1, sb2, q2, t2)
     for d in (0, 1, 3, 2):
         grad_rank(chips[d], other)
+    earlier = list(pending)
+    pending.clear()
     grad_first()
     d_residual(0)
     d_residual(1)
     grad_middle()
+    for wait in earlier:
+        wait()
 
     all_to_all_wait(2, a3s, a3r)
     weighted = (a3r[...].reshape(TOK, CH).astype(F32) * tout).astype(BF16)
@@ -585,19 +599,19 @@
     grad_second()
     drain()
 
+    all_to_all_wait(3, a4s, a4r)
+    scaled = (a4r[...].reshape(TOK, CH).astype(F32) * tin).astype(BF16)
+    d_mix = mm(scaled, bm_ref[...], 0, 1)
+    din_ref[...] = (dres_s[...].astype(F32) + d_mix).astype(BF16)
+
+    store(1, din_ref, din_hbm)
+
     rows_y = second_sum(0, y2s, y2r, z)
     rows_z = second_sum(1, z2s, z2r, y)
     gd_ref[:, 0:LANES] = rows_y[0:ROWS]
     gd_ref[:, LANES : 2 * LANES] = rows_z[0:ROWS]
     gd_ref[:, 2 * LANES : HID] = rows_y[ROWS:48] + rows_z[ROWS:48]
     store(2, gd_ref, gd_hbm)
-
-    all_to_all_wait(3, a4s, a4r)
-    scaled = (a4r[...].reshape(TOK, CH).astype(F32) * tin).astype(BF16)
-    d_mix = mm(scaled, bm_ref[...], 0, 1)
-    din_ref[...] = (dres_s[...].astype(F32) + d_mix).astype(BF16)
-
-    store(1, din_ref, din_hbm)
 
     drain()
 
@@ -640,13 +654,13 @@
             pltpu.VMEM((D, HID), BF16),
             pltpu.VMEM((D, HID), BF16),
             pltpu.VMEM((D, HID), BF16),
-            pltpu.VMEM((4, 2 * HID, HID), BF16),
-            pltpu.VMEM((4, HID, HID), BF16),
+            pltpu.VMEM((NTEN, 2 * HID, CH), BF16),
+            pltpu.VMEM((NTEN, HID, CH), BF16),
             pltpu.VMEM((NSEQ * LINE, TOK), BF16),
             pltpu.VMEM((TOK, TOK), BF16),
         ]
         + [pltpu.VMEM((8, LINE, CH), BF16)] * 2
-        + [pltpu.VMEM((NSEQ, LINE, CH), BF16)] * 2
+        + [pltpu.VMEM((NSEQ, PACKED, LANES), BF16)] * 2
         + [chunks] * 4
         + [
             pltpu.VMEM((2, NTEN, CH, HT), BF16),

time: 84.8 us -> 83.1 us (0.980)
  the two profiles are of different devices: /device:TPU:128 before, /device:TPU:1 now
where the time goes in v5:
time: 83.1 us; the launch traced here: 81.8 us
  Pallas kernels  81.1 us (98%)
    pallas_call x1, Pallas kernels, body(): pl.pallas_call(kernel, out_shape=results, in_specs=[hbm] * 10, out_specs=...  79.5 us

profile of v5, /device:TPU:1, one launch (start us, length us, event | category | flops | bytes accessed | tf_op | source)
XLA Modules:
  0.0 81.8 jit_solution(8524793445404094115)
XLA Ops:
  0.6 79.5 %monarch_block.1 = (bf16[192,256]{1,0:T(8,128)(2,1)}, bf16[192,256]{1,0:T(8,128)(2,1)}, f32[24,384]{1,0:T(8,128)}) custom-call(bf16[192,256]{1,0:T(8,128)(2,1)} %bitcast.13, bf16[192,256]{1,0:T(8,128)(2,1)} %bitcast.14, bf16[256,256]{1,0:T(8,128)(2,1)} %bm_hbm.1, bf16[16,16]{1,0:T(8,128)(2,1)} %cm_hbm.1, f32[1,256]{1,0:T(1,128)} %ti_hbm.1, f32[16,16]{1,0:T(8,128)} %to_hbm.1, ...), custom_call_target="tpu_custom_call" | custom-call | tf_op jit(solution)/shard_map/monarch_block/pallas_call | solution.py:638
  80.1 1.6 %hand_over.1 = (bf16[192,256]{1,0:T(8,128)(2,1)}, bf16[192,256]{1,0:T(8,128)(2,1)}, f32[24,384]{1,0:T(8,128)}) custom-call(bf16[192,256]{1,0:T(8,128)(2,1)} %get-tuple-element.9.out_in, bf16[192,256]{1,0:T(8,128)(2,1)} %get-tuple-element.10.din_in, f32[24,384]{1,0:T(8,128)} %get-tuple-element.11.gd_in), custom_call_target="tpu_custom_call" | custom-call | tf_op jit(solution)/shard_map/hand_over/pallas_call | solution.py:725

commit v6 on v5

--- a/solution.py
+++ b/solution.py
@@ -330,7 +330,7 @@
             if then is not None:
                 then(src // 2, c)
 
-    def gather_matmul(n, h, buf, weights):
+    def gather_matmul(n, h, buf, weights, own_seen=False):
         acc = None
         for d in (0, 1, 3, 2):
             rank = lax.rem(x + 4 - d, 4) * 2 + c
@@ -338,7 +338,8 @@
             acc = term if acc is None else acc + term
         for d in (0, 1, 3, 2):
             rank = lax.rem(x + 4 - d, 4) * 2 + other
-            wait_recv(buf.at[h, rank], sib_ss.at[n, d, h], sib_rs.at[n, d, h])
+            if d or not own_seen:
+                wait_recv(buf.at[h, rank], sib_ss.at[n, d, h], sib_rs.at[n, d, h])
             acc = acc + mm(weights[rank], buf[h, rank])
         return acc
 
@@ -386,7 +387,7 @@
         out_ref[:, halves[h]] = summed.astype(BF16)
 
     def backward(h):
-        d_hidden = gather_matmul(1, h, r2, wdT)
+        d_hidden = gather_matmul(1, h, r2, wdT, own_seen=True)
         gate_pre = gate_s[h]
         up_pre = up_s[h]
         sig = jax.nn.sigmoid(gate_pre)
@@ -573,6 +574,9 @@
     cotangent(1)
     store(0, out_ref, out_hbm)
     grad_rank(x, c)
+    for h in range(2):
+        wait_recv(r2.at[h, x * 2 + other], sib_ss.at[1, 0, h], sib_rs.at[1, 0, h])
+    grad_rank(x, other)
     gather_forward(1, 0, r2)
     backward(0)
     gather_forward(1, 1, r2)
@@ -581,7 +585,7 @@
     for d in (1, 3, 2):
         grad_rank(chips[d], c)
     scatter_mid(1, 1, sb2, q2, t2)
-    for d in (0, 1, 3, 2):
+    for d in (1, 3, 2):
         grad_rank(chips[d], other)
     earlier = list(pending)
     pending.clear()
@@ -616,17 +620,23 @@
     drain()
 
 
-def finish(out_in, din_in, gd_in, out_ref, din_ref, gd_ref):
-    out_ref[...] = out_in[...]
-    din_ref[...] = din_in[...]
-    gd_ref[...] = gd_in[...]
+def finish(*refs):
+    came, gone, held, sems = refs[0:3], refs[3:6], refs[6:9], refs[9]
+    reads = [pltpu.make_async_copy(came[n], held[n], sems.at[0, n]) for n in range(3)]
+    writes = [pltpu.make_async_copy(held[n], gone[n], sems.at[1, n]) for n in range(3)]
+    for cp in reads:
+        cp.start()
+    for n in range(3):
+        reads[n].wait()
+        writes[n].start()
+    for cp in writes:
+        cp.wait()
 
 
 def body(
     inputs, targets, block_mix, cross_mix, twiddle_in, twiddle_out, norm_gain, w_gate, w_up, w_down
 ):
     hbm = pl.BlockSpec(memory_space=pltpu.HBM)
-    vmem = pl.BlockSpec(memory_space=pltpu.VMEM)
     dma = pltpu.SemaphoreType.DMA
     chunks = pltpu.VMEM((NSEQ, POS, CH), BF16)
     blocks4 = pltpu.VMEM((2, 4, CH, HT), BF16)
@@ -725,8 +735,14 @@
     output, d_input, grad_down = pl.pallas_call(
         finish,
         out_shape=results,
-        in_specs=[vmem] * 3,
-        out_specs=(vmem, vmem, vmem),
+        in_specs=[hbm] * 3,
+        out_specs=(hbm, hbm, hbm),
+        scratch_shapes=[
+            pltpu.VMEM((CH, TOK), BF16),
+            pltpu.VMEM((CH, TOK), BF16),
+            pltpu.VMEM((ROWS, HID), F32),
+            dma((2, 3)),
+        ],
         compiler_params=pltpu.CompilerParams(vmem_limit_bytes=64 * 1024 * 1024),
         name="hand_over",
     )(*made)

time: 83.1 us -> 82.8 us (level)
  no operation moved by 1% of the time
where the time goes in v6:
time: 82.8 us; the launch traced here: 81.4 us
  Pallas kernels  80.7 us (97%)
    pallas_call x1, Pallas kernels, body(): pl.pallas_call(kernel, out_shape=results, in_specs=[hbm] * 10, out_specs=...  79.1 us

profile of v6, /device:TPU:1, one launch (start us, length us, event | category | flops | bytes accessed | tf_op | source)
XLA Modules:
  0.0 81.4 jit_solution(2695328992424612325)
XLA Ops:
  0.6 79.1 %monarch_block.1 = (bf16[192,256]{1,0:T(8,128)(2,1)}, bf16[192,256]{1,0:T(8,128)(2,1)}, f32[24,384]{1,0:T(8,128)}) custom-call(bf16[192,256]{1,0:T(8,128)(2,1)} %bitcast.13, bf16[192,256]{1,0:T(8,128)(2,1)} %bitcast.14, bf16[256,256]{1,0:T(8,128)(2,1)} %bm_hbm.1, bf16[16,16]{1,0:T(8,128)(2,1)} %cm_hbm.1, f32[1,256]{1,0:T(1,128)} %ti_hbm.1, f32[16,16]{1,0:T(8,128)} %to_hbm.1, ...), custom_call_target="tpu_custom_call" | custom-call | tf_op jit(solution)/shard_map/monarch_block/pallas_call | solution.py:648
  79.7 1.6 %hand_over.1 = (bf16[192,256]{1,0:T(8,128)(2,1)}, bf16[192,256]{1,0:T(8,128)(2,1)}, f32[24,384]{1,0:T(8,128)}) custom-call(bf16[192,256]{1,0:T(8,128)(2,1)} %get-tuple-element.9.refs_0_, bf16[192,256]{1,0:T(8,128)(2,1)} %get-tuple-element.10.refs_1_, f32[24,384]{1,0:T(8,128)} %get-tuple-element.11.refs_2_), custom_call_target="tpu_custom_call" | custom-call | tf_op jit(solution)/shard_map/hand_over/pallas_call | solution.py:735

commit v7 on v6

--- a/solution.py
+++ b/solution.py
@@ -49,7 +49,7 @@
     wg, wu, wd, wguT, wdT, kron, kronT,
     a1s, a1r, a2s, a2r, a3s, a3r, a4s, a4r,
     r1, r2, v1, v2,
-    p1, p2, sb1, sb2, q1, q2, t1, t2, own, gate_s, up_s, hid_s, res_s, dres_s,
+    p1, p2, sb1, sb2, q1, q2, t1, t2, own, pre_s, back_s, gate_s, up_s, hid_s, res_s, dres_s,
     ya, yr, zb, zr, y2s, y2r, z2s, z2r,
     to_pair, cross_sem, tw_sem, osem, wsem, a_ss, a_rs, ag_ss, ag_rs, sib_ss, sib_rs, v_ss, v_rs,
     rsib_ss, rsib_rs, rs_ss, rs_rs, g_ss, g_rs, g2_ss, g2_rs,
@@ -330,18 +330,22 @@
             if then is not None:
                 then(src // 2, c)
 
-    def gather_matmul(n, h, buf, weights, own_seen=False):
-        acc = None
-        for d in (0, 1, 3, 2):
+    def gather_own(n, h, buf, weights, acc):
+        rank = x * 2 + other
+        first = mm(weights[tn], buf[h, tn])
+        wait_recv(buf.at[h, rank], sib_ss.at[n, 0, h], sib_rs.at[n, 0, h])
+        acc[h] = first + mm(weights[rank], buf[h, rank])
+
+    def gather_matmul(n, h, buf, weights, acc):
+        total = acc[h]
+        for d in (1, 3, 2):
             rank = lax.rem(x + 4 - d, 4) * 2 + c
-            term = mm(weights[rank], buf[h, rank])
-            acc = term if acc is None else acc + term
-        for d in (0, 1, 3, 2):
+            total = total + mm(weights[rank], buf[h, rank])
+        for d in (1, 3, 2):
             rank = lax.rem(x + 4 - d, 4) * 2 + other
-            if d or not own_seen:
-                wait_recv(buf.at[h, rank], sib_ss.at[n, d, h], sib_rs.at[n, d, h])
-            acc = acc + mm(weights[rank], buf[h, rank])
-        return acc
+            wait_recv(buf.at[h, rank], sib_ss.at[n, d, h], sib_rs.at[n, d, h])
+            total = total + mm(weights[rank], buf[h, rank])
+        return total
 
     def scatter_start(n, h, part_of, p, sb):
         for d in (2, 1, 3, 0):
@@ -370,7 +374,7 @@
     inv = [None, None]
 
     def forward(h):
-        pre = gather_matmul(0, h, r1, wguT)
+        pre = gather_matmul(0, h, r1, wguT, pre_s)
         inv[h] = lax.rsqrt(sum_rows(0, h, v1) / D + EPS)
         gate_pre = pre[0:HID] * inv[h]
         up_pre = pre[HID : 2 * HID] * inv[h]
@@ -387,7 +391,7 @@
         out_ref[:, halves[h]] = summed.astype(BF16)
 
     def backward(h):
-        d_hidden = gather_matmul(1, h, r2, wdT, own_seen=True)
+        d_hidden = gather_matmul(1, h, r2, wdT, back_s)
         gate_pre = gate_s[h]
         up_pre = up_s[h]
         sig = jax.nn.sigmoid(gate_pre)
@@ -564,6 +568,8 @@
 
     residual(0)
     residual(1)
+    gather_own(0, 0, r1, wguT, pre_s)
+    gather_own(0, 1, r1, wguT, pre_s)
     gather_forward(0, 0, r1)
     forward(0)
     gather_forward(0, 1, r1)
@@ -574,8 +580,8 @@
     cotangent(1)
     store(0, out_ref, out_hbm)
     grad_rank(x, c)
-    for h in range(2):
-        wait_recv(r2.at[h, x * 2 + other], sib_ss.at[1, 0, h], sib_rs.at[1, 0, h])
+    gather_own(1, 0, r2, wdT, back_s)
+    gather_own(1, 1, r2, wdT, back_s)
     grad_rank(x, other)
     gather_forward(1, 0, r2)
     backward(0)
@@ -681,6 +687,8 @@
         + [blocks4] * 8
         + [
             pltpu.VMEM((2, 4, CH, HT), F32),
+            pltpu.VMEM((2, 2 * HID, HT), F32),
+            pltpu.VMEM((2, HID, HT), F32),
             pltpu.VMEM((2, HID, HT), F32),
             pltpu.VMEM((2, HID, HT), F32),
             pltpu.VMEM((2, HID, HT), BF16),

time: 82.8 us -> 82.3 us (level)
  no operation moved by 1% of the time
where the time goes in v7:
time: 82.3 us; the launch traced here: 81 us
  Pallas kernels  80.3 us (98%)
    pallas_call x1, Pallas kernels, body(): pl.pallas_call(kernel, out_shape=results, in_specs=[hbm] * 10, out_specs=...  78.7 us

profile of v7, /device:TPU:1, one launch (start us, length us, event | category | flops | bytes accessed | tf_op | source)
XLA Modules:
  0.0 81.0 jit_solution(17111673726026277917)
XLA Ops:
  0.6 78.7 %monarch_block.1 = (bf16[192,256]{1,0:T(8,128)(2,1)}, bf16[192,256]{1,0:T(8,128)(2,1)}, f32[24,384]{1,0:T(8,128)}) custom-call(bf16[192,256]{1,0:T(8,128)(2,1)} %bitcast.13, bf16[192,256]{1,0:T(8,128)(2,1)} %bitcast.14, bf16[256,256]{1,0:T(8,128)(2,1)} %bm_hbm.1, bf16[16,16]{1,0:T(8,128)(2,1)} %cm_hbm.1, f32[1,256]{1,0:T(1,128)} %ti_hbm.1, f32[16,16]{1,0:T(8,128)} %to_hbm.1, ...), custom_call_target="tpu_custom_call" | custom-call | tf_op jit(solution)/shard_map/monarch_block/pallas_call | solution.py:654
  79.3 1.6 %hand_over.1 = (bf16[192,256]{1,0:T(8,128)(2,1)}, bf16[192,256]{1,0:T(8,128)(2,1)}, f32[24,384]{1,0:T(8,128)}) custom-call(bf16[192,256]{1,0:T(8,128)(2,1)} %get-tuple-element.9.refs_0_, bf16[192,256]{1,0:T(8,128)(2,1)} %get-tuple-element.10.refs_1_, f32[24,384]{1,0:T(8,128)} %get-tuple-element.11.refs_2_), custom_call_target="tpu_custom_call" | custom-call | tf_op jit(solution)/shard_map/hand_over/pallas_call | solution.py:743

commit v8 on v7

--- a/solution.py
+++ b/solution.py
@@ -209,7 +209,9 @@
 
     rows_here = flags(iota((8, NSEQ), 1) == 2 * iota((8, NSEQ), 0) + zh)
     cross_here = mm(rows_here, cross).astype(BF16)
-    wide = mm(flags(iota((NSEQ * LINE, NSEQ), 0) // LINE == iota((NSEQ * LINE, NSEQ), 1)), cross_here, 1, 1)
+    place = iota((NSEQ * LINE, NSEQ), 0)
+    block = 2 * (place % TOK // LINE) + jnp.where(place < TOK, 1 - zh, zh)
+    wide = mm(flags(block == iota((NSEQ * LINE, NSEQ), 1)), cross_here, 1, 1)
     wide = mm(wide.astype(BF16), flags(iota((8, TOK), 1) // LINE == iota((8, TOK), 0)))
     same_pos = iota((NSEQ * LINE, TOK), 0) % LINE == iota((NSEQ * LINE, TOK), 1) % LINE
     kron[...] = jnp.where(same_pos, wide, 0.0).astype(BF16)
@@ -258,13 +260,22 @@
         peer = lax.rem(y + i, 8)
         wait_recv(a1r.at[peer], a_ss.at[0, peer], a_rs.at[0, peer])
 
-    mixed = mm(kron[...], a1r[...].reshape(TOK, CH)) * tline
-    mixed = mixed.reshape(NSEQ, LINE, CH)
-    a2s[:, 0:LINE, :] = mixed[:, :, 0:LANES].astype(BF16)
-    rest = mixed[:, :, LANES:CH]
-    rest = jnp.concatenate([rest[:, 0:POS], rest[:, POS:LINE]], axis=2)
-    a2s[:, LINE:PACKED, :] = rest.astype(BF16)
-    all_to_all_send(1, a2s, a2r)
+    tline = tline.reshape(8, 2, LINE, 1)
+    for own_line in range(2):
+        part = zh if own_line else 1 - zh
+        tw = jnp.where(part == 0, tline[:, 0], tline[:, 1]).reshape(TOK, 1)
+        mixed = mm(kron[own_line * TOK : own_line * TOK + TOK, :], a1r[...].reshape(TOK, CH)) * tw
+        mixed = mixed.reshape(8, LINE, CH)
+        rest = mixed[:, :, LANES:CH]
+        rest = jnp.concatenate([rest[:, 0:POS], rest[:, POS:LINE]], axis=2).astype(BF16)
+        mixed = mixed[:, :, 0:LANES].astype(BF16)
+        for ky in range(8):
+            a2s[ky * 2 + part, 0:LINE, :] = mixed[ky]
+            a2s[ky * 2 + part, LINE:PACKED, :] = rest[ky]
+        for i in FAR_FIRST + (() if own_line else (0,)):
+            a2a_copy(1, a2s, a2r, lax.rem(y + i, 8) * 2 + part).start()
+    a2r[sq] = a2s[sq]
+    pending.append(functools.partial(all_to_all_done, 1, a2s, a2r))
 
     halves = [slice(0, HT), slice(HT, TOK)]
 

time: 82.3 us -> 81.1 us (0.985); the launches traced: 81 us -> 81 us
  no operation moved by 1% of the time
where the time goes in v8:
time: 81.1 us; the launch traced here: 81 us
  Pallas kernels  80.2 us (99%)
    pallas_call x1, Pallas kernels, body(): pl.pallas_call(kernel, out_shape=results, in_specs=[hbm] * 10, out_specs=...  78.5 us
    pallas_call x1, Pallas kernels, body(): pl.pallas_call(finish, out_shape=results, in_specs=[hbm] * 3, out_specs=(...  1.64 us

profile of v8, /device:TPU:1, one launch (start us, length us, event | category | flops | bytes accessed | tf_op | source)
XLA Modules:
  0.0 81.0 jit_solution(12746385914780310675)
XLA Ops:
  0.6 78.5 %monarch_block.1 = (bf16[192,256]{1,0:T(8,128)(2,1)}, bf16[192,256]{1,0:T(8,128)(2,1)}, f32[24,384]{1,0:T(8,128)}) custom-call(bf16[192,256]{1,0:T(8,128)(2,1)} %bitcast.13, bf16[192,256]{1,0:T(8,128)(2,1)} %bitcast.14, bf16[256,256]{1,0:T(8,128)(2,1)} %bm_hbm.1, bf16[16,16]{1,0:T(8,128)(2,1)} %cm_hbm.1, f32[1,256]{1,0:T(1,128)} %ti_hbm.1, f32[16,16]{1,0:T(8,128)} %to_hbm.1, ...), custom_call_target="tpu_custom_call" | custom-call | tf_op jit(solution)/shard_map/monarch_block/pallas_call | solution.py:665
  79.2 1.6 %hand_over.1 = (bf16[192,256]{1,0:T(8,128)(2,1)}, bf16[192,256]{1,0:T(8,128)(2,1)}, f32[24,384]{1,0:T(8,128)}) custom-call(bf16[192,256]{1,0:T(8,128)(2,1)} %get-tuple-element.9.refs_0_, bf16[192,256]{1,0:T(8,128)(2,1)} %get-tuple-element.10.refs_1_, f32[24,384]{1,0:T(8,128)} %get-tuple-element.11.refs_2_), custom_call_target="tpu_custom_call" | custom-call | tf_op jit(solution)/shard_map/hand_over/pallas_call | solution.py:754
